TPU v7x, 512 devices: a whole 4x8x8 slice. The times are simulated.
512 devices in a mesh: rep: 64 (over z, y_hi, core), mp: 8 (over y_lo, x).
Axes of the slice: x: 4, y: 8 (y_hi: 4, y_lo: 2; y = y_hi * 2 + y_lo), z: 8, core: 2. Of those that a mesh axis runs over, the one named last changes fastest.
Arguments:
- momentum: float32 [64, 2, 128, 5120], P('rep', None, None, 'mp'), may hold values from -6 to 6
- gradient: bfloat16 [64, 2, 128, 5120], P('rep', None, None, 'mp')
- kept_index: int32 [64], replicated, may hold values from 0 to 4095, as said below
Outputs:
- new_momentum: float32 [64, 2, 128, 5120], P('rep', None, None, 'mp')
- update: bfloat16 [2, 128, 5120], P(None, None, 'mp')
Inputs may be any that keep to these rules, and one draw needn't show every extreme that they name: `kept_index`: 64 distinct indices u * 64 + v, for row frequency u and column frequency v.
All inputs are finite; a program needn't handle non-finite values. Where the computation divides by a largest or mean magnitude, that divisor is 1e-20 or more.
Results may differ from a plain program's by a relative error of at most 0.001.
Values sent between devices are 32-bit elements; how exact they have to be, the bound alone decides.
No kernel may reach another device: no remote copies, remote signals or barrier semaphores. Data moves between devices by JAX's collectives and lax.ppermute only.
A program may use at most 64 MiB of HBM per device.

v0:
```python
import math

import jax
import jax.numpy as jnp
from jax import lax
from jax.sharding import PartitionSpec as P

GROUP = 64


decay_rate = 0.999
epsilon = 1e-06
precise = lax.Precision.HIGHEST


def dct_matrix(order):
    freq = jnp.arange(order)[:, None]
    place = jnp.arange(order)[None, :]
    cosines = jnp.cos(jnp.pi * (2 * place + 1) * freq / (2 * order))
    scales = jnp.where(freq == 0, math.sqrt(1.0 / order), math.sqrt(2.0 / order))
    return (cosines * scales).astype(jnp.float32)


def collect(flattened):
    shared = lax.psum_scatter(flattened, "rep", scatter_dimension=0, tiled=True)
    return lax.all_gather(shared, "rep", axis=0, tiled=True)


def per_device(momentum, gradient, kept_index):
    layer_count = momentum.shape[1]
    row_count = momentum.shape[2]
    col_count = momentum.shape[3]
    cosines = dct_matrix(GROUP)
    positions = jnp.arange(GROUP)
    row_pick = (kept_index[:, None] // GROUP == positions[None, :]).astype(jnp.float32)
    col_pick = (kept_index[:, None] % GROUP == positions[None, :]).astype(jnp.float32)
    row_c = jnp.dot(row_pick, cosines, precision=precise)
    col_c = jnp.dot(col_pick, cosines, precision=precise)

    def decode(spectra):
        return jnp.einsum("lacj,jm,jn->lamcn", spectra, row_c, col_c, precision=precise)

    grad_wide = gradient[0].astype(jnp.float32)
    squares = jnp.sum(grad_wide * grad_wide, axis=(1, 2))
    sum_squares = lax.psum(squares, "mp")
    mean_square = sum_squares / (row_count * col_count * lax.axis_size("mp"))
    clip = 1.0 / jnp.maximum(1.0, jnp.sqrt(mean_square + epsilon))
    moment = decay_rate * momentum[0] + clip[:, None, None] * grad_wide
    blocks = moment.reshape(layer_count, row_count // GROUP, GROUP, col_count // GROUP, GROUP)
    spectra = jnp.einsum("lamcn,jm,jn->lacj", blocks, row_c, col_c, precision=precise)
    own_part = decode(spectra)
    new_momentum = (blocks - own_part).reshape(1, layer_count, row_count, col_count)
    flattened = spectra.reshape(layer_count, -1)
    totals = jnp.stack([collect(flattened[layer]) for layer in range(layer_count)])
    totals = totals.reshape(spectra.shape)
    decoded = decode(totals)
    magnitude = jnp.mean(jnp.abs(decoded), axis=(2, 4), keepdims=True)
    update = jnp.tanh(decoded / (magnitude + epsilon)).reshape(layer_count, row_count, col_count)
    return (new_momentum, update.astype(jnp.bfloat16))


def solution(mesh):
    return jax.shard_map(
        per_device,
        mesh=mesh,
        in_specs=(P("rep", None, None, "mp"), P("rep", None, None, "mp"), P()),
        out_specs=(P("rep", None, None, "mp"), P(None, None, "mp")),
        check_vma=False,
    )
```

profile of v0, /device:TPU:1, one launch (start us, length us, event | category | flops | bytes accessed | tf_op | source)
XLA Modules:
  0.0 591.3 jit_solution(13422818881637106695)
XLA Ops:
  0.6 0.0 copy-start.1
  0.6 1.5 reshape.100
  2.2 0.0 copy-done.1
  2.2 0.1 broadcast_multiply_fusion
  2.3 0.0 copy-start
  2.3 1.8 reshape.99
  4.1 0.0 copy-done
  4.1 0.2 multiply_reduce_fusion
  4.3 16.8 %psum.7 = f32[2]{0:T(128)S(1)} all-reduce(f32[2]{0:T(128)S(1)} %multiply_reduce_fusion), channel_id=1, replica_groups=mesh['rep'=64,'mp'=8] {'mp'}, use_global_device_ids=true, to_apply=%region_1.2 | all-reduce | flops 2 | bytes 16 | tf_op jit(solution)/shard_map/psum | solution.py:45
  21.1 2.4 fusion.5
  23.5 0.0 copy-done.3
  23.5 0.4 fusion.19
  23.9 0.3 fusion.18
  24.3 2.6 fusion
  26.8 1.2 fusion.4
  28.0 0.8 copy.38
  28.8 0.0 copy-start.2
  28.8 1.3 reshape.101
  30.1 0.0 copy-done.2
  30.1 0.7 fusion.33
  31.5 0.1 squeeze.9
  31.6 0.1 squeeze.8
  31.6 280.3 %all-reduce.5 = (f32[1280]{0:T(1024)S(1)}, f32[1280]{0:T(1024)S(1)}) all-reduce(f32[1280]{0:T(1024)S(1)} %squeeze.9, f32[1280]{0:T(1024)S(1)} %squeeze.8), channel_id=3, replica_groups=mesh['rep'=64,'mp'=8] {'rep'}, use_global_device_ids=true, to_apply=%region_3.4.clone | all-reduce | flops 2560 | bytes 20480
  312.6 0.2 dynamic-slice_dynamic-update-slice_fusion
  312.8 0.2 dynamic-slice_dynamic-update-slice_fusion.1
  312.9 274.9 %all-reduce.4 = (f32[1280]{0:T(1024)S(1)}, f32[1280]{0:T(1024)S(1)}) all-reduce(f32[1280]{0:T(1024)S(1)} %dynamic-slice_dynamic-update-slice_fusion, f32[1280]{0:T(1024)S(1)} %dynamic-slice_dynamic-update-slice_fusion.1), channel_id=1, replica_groups=mesh['rep'=64,'mp'=8] {'rep'}, use_global_device_ids=true, to_apply=%add.1 | all-reduce | flops 2560 | bytes 20480
  587.8 0.1 stack.12
  587.9 0.1 stack.11
  588.0 1.3 abs_reduce_fusion
  589.3 0.3 fusion.15
  589.6 0.5 copy.39
  590.0 1.3 reshape.102
  (10 shorter events, 0.1 us)
Async XLA Ops:
  0.6 1.6 copy-start.1
  2.3 1.8 copy-start
  21.1 2.4 copy-start.3
  28.8 1.3 copy-start.2
where the time goes:
time: 596 us; the launch traced here: 591 us
  blocking collectives  572 us (96%)
  local copies, waits for them, and re-layouts  8.53 us (1%)
    unnamed x2, blocking collectives  555 us
    psum x1, blocking collectives, per_device(): sum_squares = lax.psum(squares, 'mp')  16.8 us

commit v1 on v0

v1 whole, which is shorter than its diff:
```python
import math

import jax
import jax.numpy as jnp
import ml_dtypes
import numpy as np
from jax import lax
from jax.experimental import pallas as pl
from jax.experimental.pallas import tpu as pltpu
from jax.sharding import Mesh, PartitionSpec as P

GROUP = 64
LANES = 128
decay_rate = 0.999
epsilon = 1e-06
f32 = jnp.float32
bf16 = jnp.bfloat16
PARAMS = pltpu.CompilerParams(vmem_limit_bytes=24 * 1024 * 1024)


def dct_parts():
    freq = np.arange(GROUP)[:, None]
    place = np.arange(GROUP)[None, :]
    cosines = np.cos(np.pi * (2 * place + 1) * freq / (2 * GROUP))
    scales = np.where(freq == 0, math.sqrt(1.0 / GROUP), math.sqrt(2.0 / GROUP))
    rest = (cosines * scales).astype(np.float32).T
    parts = []
    for _ in range(3):
        part = rest.astype(ml_dtypes.bfloat16)
        parts.append(part)
        rest = rest - part.astype(np.float32)
    return parts


def halves(x):
    high = x.astype(bf16)
    return high, (x - high.astype(f32)).astype(bf16)


def times(x, b_high, b_low, transposed):
    dims = (((1,), (1 if transposed else 0,)), ((), ()))
    x_high, x_low = halves(x)
    dot = lambda a, b: lax.dot_general(a, b, dims, preferred_element_type=f32)
    return dot(x_high, b_high) + (dot(x_high, b_low) + dot(x_low, b_high))


def first_kernel(grad_ref, kept_ref, row_ref, col_ref, squares_ref, pick_ref, high_ref, low_ref):
    layers = grad_ref.shape[1]
    blocks = grad_ref.shape[3] // LANES
    rows = []
    for layer in range(layers):
        total = None
        for b in range(blocks):
            g = grad_ref[0, layer, :, b * LANES : (b + 1) * LANES].astype(f32)
            part = jnp.sum((g * g).reshape(-1, 8, LANES), axis=0)
            total = part if total is None else total + part
        rows.append(total[0:4] + total[4:8])
    part = jnp.concatenate(rows, axis=0)
    squares_ref[...] = jnp.broadcast_to(part[None], squares_ref.shape)

    kept = kept_ref[...]
    place = lax.broadcasted_iota(jnp.int32, (GROUP, LANES), 0)
    lane = lax.broadcasted_iota(jnp.int32, (GROUP, LANES), 1)
    row_hot = jnp.where(place == (kept >> 6), 1.0, 0.0).astype(bf16)
    col_hot = jnp.where(place == (kept & 63), 1.0, 0.0).astype(bf16)
    pick = None
    for i in range(3):
        term = jnp.dot(row_ref[i], row_hot, preferred_element_type=f32)
        pick = term if pick is None else pick + term
    pick_ref[...] = pick
    for i, ref in enumerate((high_ref, low_ref)):
        part = jnp.dot(col_ref[i], col_hot, preferred_element_type=f32)
        ref[...] = jnp.concatenate(
            [jnp.where(lane < GROUP, part, 0.0), jnp.where(lane < GROUP, 0.0, part)], axis=0
        ).astype(bf16)


def clips(squares_ref, layers, count):
    total = jnp.sum(squares_ref[...], axis=0)
    each = 8 // layers
    out = []
    for layer in range(layers):
        square = jnp.sum(total[layer * each : (layer + 1) * each], keepdims=True)
        out.append(1.0 / jnp.maximum(1.0, jnp.sqrt(square / count + epsilon)))
    return out


def moment_block(mom_ref, grad_ref, clip, b):
    lanes = slice(b * LANES, (b + 1) * LANES)
    return jnp.concatenate(
        [
            decay_rate * mom_ref[0, layer, :, lanes] + clip[layer] * grad_ref[0, layer, :, lanes].astype(f32)
            for layer in range(len(clip))
        ],
        axis=0,
    )


def encode_kernel(count, mom_ref, grad_ref, squares_ref, pick_ref, high_ref, low_ref, out_ref):
    layers = grad_ref.shape[1]
    blocks = grad_ref.shape[3] // LANES
    clip = clips(squares_ref, layers, count)
    pick = pick_ref[...]
    spectra = []
    for b in range(blocks):
        x = moment_block(mom_ref, grad_ref, clip, b)
        t = times(x, high_ref[...], low_ref[...], False)
        spectra.append(jnp.sum(t.reshape(-1, GROUP, LANES) * pick[None], axis=1))
    spectra.append(jnp.zeros_like(spectra[0]))
    half = len(spectra) // 2
    for i in range(half):
        both = jnp.concatenate([spectra[i], spectra[half + i]], axis=0)
        out_ref[:, :, i * LANES : (i + 1) * LANES] = jnp.broadcast_to(both[None], (out_ref.shape[0], 8, LANES))


def decode_block(spectra, pick, b_high, b_low):
    wide = (spectra[:, None, :] * pick[None]).reshape(-1, LANES)
    return times(wide, b_high, b_low, True)


def last_kernel(count, mom_ref, grad_ref, squares_ref, own_ref, total_ref, pick_ref, high_ref, low_ref, new_ref, update_ref):
    layers, rows = grad_ref.shape[1:3]
    blocks = grad_ref.shape[3] // LANES
    half = (blocks + 1) // 2
    clip = clips(squares_ref, layers, count)
    pick = pick_ref[...]
    b_high, b_low = high_ref[...], low_ref[...]
    own = own_ref[0]
    total = jnp.sum(total_ref[...], axis=0)

    def block(packed, b):
        lanes = slice((b % half) * LANES, (b % half + 1) * LANES)
        return packed[4:8, lanes] if b >= half else packed[0:4, lanes]

    lane = lax.broadcasted_iota(jnp.int32, (4, LANES), 1)
    for b in range(blocks):
        lanes = slice(b * LANES, (b + 1) * LANES)
        x = moment_block(mom_ref, grad_ref, clip, b)
        new = x - decode_block(block(own, b), pick, b_high, b_low)
        for layer in range(layers):
            new_ref[0, layer, :, lanes] = new[layer * rows : (layer + 1) * rows]
        d = decode_block(block(total, b), pick, b_high, b_low)
        tiles = d.reshape(4, GROUP, LANES)
        size = jnp.sum(jnp.abs(tiles), axis=1)
        left = jnp.sum(jnp.where(lane < GROUP, size, 0.0), axis=1, keepdims=True)
        right = jnp.sum(jnp.where(lane < GROUP, 0.0, size), axis=1, keepdims=True)
        mean = jnp.where(lane < GROUP, left, right) / (GROUP * GROUP)
        scale = 1.0 / (mean + epsilon)
        update = jnp.tanh(tiles * scale[:, None, :]).astype(bf16).reshape(layers, rows, LANES)
        update_ref[:, :, lanes] = update


def exchange(x, axes):
    return lax.all_to_all(x, axes, 0, 0, tiled=True)


def solution(mesh):
    whole = Mesh(mesh.devices.reshape(8, 4, 2, 2, 4), ("z", "yh", "core", "yl", "x"))
    rep, mp = ("z", "yh", "core"), ("yl", "x")
    parts = dct_parts()
    three = np.stack(parts)
    two = np.stack(parts[:2])

    def per_device(momentum, gradient, kept_index):
        _, layers, rows, cols = momentum.shape
        count = float(rows * cols * 8)
        kept = jnp.concatenate([kept_index, kept_index]).reshape(1, LANES)
        sds = jax.ShapeDtypeStruct
        squares, pick, high, low = pl.pallas_call(
            first_kernel,
            out_shape=(
                sds((8, 8, LANES), f32),
                sds((GROUP, LANES), f32),
                sds((LANES, LANES), bf16),
                sds((LANES, LANES), bf16),
            ),
            compiler_params=PARAMS,
            name="squares_and_picks",
        )(gradient, kept, three, two)
        squares = exchange(squares, mp)
        own = pl.pallas_call(
            lambda *refs: encode_kernel(count, *refs),
            out_shape=sds((8, 8, 3 * LANES), f32),
            compiler_params=PARAMS,
            name="encode",
        )(momentum, gradient, squares, pick, high, low)
        got = exchange(own, "z")
        some = jnp.broadcast_to(jnp.sum(got, axis=0, keepdims=True), got.shape)
        total = exchange(some, ("yh", "core"))
        return pl.pallas_call(
            lambda *refs: last_kernel(count, *refs),
            out_shape=(sds(momentum.shape, f32), sds((layers, rows, cols), bf16)),
            compiler_params=PARAMS,
            name="decode",
        )(momentum, gradient, squares, own, total, pick, high, low)

    return jax.shard_map(
        per_device,
        mesh=whole,
        in_specs=(P(rep, None, None, mp), P(rep, None, None, mp), P()),
        out_specs=(P(rep, None, None, mp), P(None, None, mp)),
        check_vma=False,
    )
```

time: 596 us -> 53.4 us (0.09)
  blocking collectives: 572 us -> 45.5 us
    unnamed x2 -> x0, blocking collectives: 555 us -> none
    all_to_all x0 -> x3, blocking collectives: none -> 45.5 us  [exchange(): return lax.all_to_all(x, axes, 0, 0, tiled=True)]
    psum x1 -> x0, blocking collectives: 16.8 us -> none  [per_device(): sum_squares = lax.psum(squares, 'mp')]
where the time goes in v1:
time: 53.4 us; the launch traced here: 53 us
  blocking collectives  45.5 us (85%)
  local copies, waits for them, and re-layouts  3.63 us (7%)
  Pallas kernels  2.43 us (5%)
  other arithmetic  0.82 us (2%)
  between operations  0.67 us (1%)
    all_to_all x3, blocking collectives, exchange(): return lax.all_to_all(x, axes, 0, 0, tiled=True)  45.5 us
    unnamed x12, local copies, waits for them, and re-layouts  3.62 us
    pallas_call x1, Pallas kernels, per_device(): pl.pallas_call(lambda *refs: last_kernel(count, *refs), out_shape=(sds(mo...  1.66 us

profile of v1, /device:TPU:1, one launch (start us, length us, event | category | flops | bytes accessed | tf_op | source)
XLA Modules:
  0.0 53.0 jit_solution(3366113261476624940)
XLA Ops:
  0.6 0.8 %add_bitcast_fusion.kept_ref = s32[1,128]{1,0:T(1,128)S(1)} fusion(s32[64]{0:T(128)} %param.7), kind=kLoop, calls=%fused_computation | loop fusion | flops 128 | bytes 768 | tf_op jit(solution)/shard_map/reshape | solution.py:167
  1.4 0.0 copy-start
  1.4 1.0 %copy-done = bf16[1,2,128,640]{3,2,1,0:T(8,128)(2,1)S(1)} copy-done((bf16[1,2,128,640]{3,2,1,0:T(8,128)(2,1)S(1)}, bf16[1,2,128,640]{3,2,1,0:T(8,128)(2,1)}, u32[]{:S(2)}) %copy-start) | copy-done | bytes 327704
  2.4 0.0 copy-start.4
  2.4 0.8 %copy-done.4 = bf16[3,64,64]{2,1,0:T(8,128)(2,1)S(1)} copy-done((bf16[3,64,64]{2,1,0:T(8,128)(2,1)S(1)}, bf16[3,64,64]{2,1,0:T(8,128)(2,1)}, u32[]{:S(2)}) %copy-start.4) | copy-done | bytes 24600
  3.2 0.0 copy-start.5
  3.2 0.8 %copy-done.5 = bf16[2,64,64]{2,1,0:T(8,128)(2,1)S(1)} copy-done((bf16[2,64,64]{2,1,0:T(8,128)(2,1)S(1)}, bf16[2,64,64]{2,1,0:T(8,128)(2,1)}, u32[]{:S(2)}) %copy-start.5) | copy-done | bytes 16408
  4.0 0.2 squares_and_picks.1
  4.2 10.8 %all_to_all.15.refs_2_ = f32[8,8,128]{2,1,0:T(8,128)S(1)} all-to-all(f32[8,8,128]{2,1,0:T(8,128)S(1)} %get-tuple-element.6), channel_id=1, replica_groups=mesh['z'=8,'yh'=4,'core'=2,'yl'=2,'x'=4] {'yl','x'}, dimensions={0} | all-to-all | bytes 65536 | tf_op jit(solution)/shard_map/all_to_all | solution.py:154
  14.9 0.0 copy-start.2
  14.9 1.1 %copy-done.2 = f32[1,2,128,640]{3,2,1,0:T(8,128)S(1)} copy-done((f32[1,2,128,640]{3,2,1,0:T(8,128)S(1)}, f32[1,2,128,640]{3,2,1,0:T(8,128)}, u32[]{:S(2)}) %copy-start.2) | copy-done | bytes 655384
  16.0 0.0 copy-start.3
  16.0 0.6 %encode.1.refs_3_ = f32[8,8,384]{2,1,0:T(8,128)S(1)} custom-call(f32[1,2,128,640]{3,2,1,0:T(8,128)S(1)} %copy-done.2, bf16[1,2,128,640]{3,2,1,0:T(8,128)(2,1)S(1)} %copy-done, f32[8,8,128]{2,1,0:T(8,128)S(1)} %all_to_all.15.refs_2_, f32[64,128]{1,0:T(8,128)S(1)} %get-tuple-element.7.refs_3_.refs_5_, bf16[128,128]{1,0:T(8,128)(2,1)S(1)} %get-tuple-element.8.refs_4_.refs_6_, ...), custom_call_target="tpu_custom_call" | custom-call | tf_op jit(solution)/shard_map/encode/pallas_call | solution.py:181
  16.6 0.0 copy-start.1
  16.6 17.5 %all_to_all.16 = f32[8,8,384]{2,1,0:T(8,128)S(1)} all-to-all(f32[8,8,384]{2,1,0:T(8,128)S(1)} %encode.1.refs_3_), channel_id=1, replica_groups=mesh['z'=8,'yh'=4,'core'=2,'yl'=2,'x'=4] {'z'}, dimensions={0} | all-to-all | bytes 196608 | tf_op jit(solution)/shard_map/all_to_all | solution.py:154
  34.2 17.2 %all_to_all.17.refs_4_ = f32[8,8,384]{2,1,0:T(8,128)S(1)} all-to-all(f32[8,8,384]{2,1,0:T(8,128)S(1)} %broadcast_in_dim.2), channel_id=1, replica_groups=mesh['z'=8,'yh'=4,'core'=2,'yl'=2,'x'=4] {'yh','core'}, dimensions={0} | all-to-all | bytes 196608 | tf_op jit(solution)/shard_map/all_to_all | solution.py:154
  51.3 0.0 copy-done.3
  51.4 0.0 copy-done.1
  51.4 1.7 %decode.1 = (f32[1,2,128,640]{3,2,1,0:T(8,128)}, bf16[2,128,640]{2,1,0:T(8,128)(2,1)}) custom-call(f32[1,2,128,640]{3,2,1,0:T(8,128)S(1)} %copy-done.3, bf16[1,2,128,640]{3,2,1,0:T(8,128)(2,1)S(1)} %copy-done.1, f32[8,8,128]{2,1,0:T(8,128)S(1)} %all_to_all.15.refs_2_, f32[8,8,384]{2,1,0:T(8,128)S(1)} %encode.1.refs_3_, f32[8,8,384]{2,1,0:T(8,128)S(1)} %all_to_all.17.refs_4_, ...), custom_call_target="tpu_custom_call" | custom-call | tf_op jit(solution)/shard_map/decode/pallas_call | solution.py:190
  (2 shorter events, 0.0 us)
Async XLA Ops:
  1.4 1.0 %copy-start = (bf16[1,2,128,640]{3,2,1,0:T(8,128)(2,1)S(1)}, bf16[1,2,128,640]{3,2,1,0:T(8,128)(2,1)}, u32[]{:S(2)}) copy-start(bf16[1,2,128,640]{3,2,1,0:T(8,128)(2,1)} %refs_1_.3) | copy-start | bytes 983044
  2.4 0.8 %copy-start.4 = (bf16[3,64,64]{2,1,0:T(8,128)(2,1)S(1)}, bf16[3,64,64]{2,1,0:T(8,128)(2,1)}, u32[]{:S(2)}) copy-start(bf16[3,64,64]{2,1,0:T(8,128)(2,1)} %constant.6.clone.row_ref) | copy-start | bytes 73732
  3.2 0.8 %copy-start.5 = (bf16[2,64,64]{2,1,0:T(8,128)(2,1)S(1)}, bf16[2,64,64]{2,1,0:T(8,128)(2,1)}, u32[]{:S(2)}) copy-start(bf16[2,64,64]{2,1,0:T(8,128)(2,1)} %constant.7.clone.col_ref) | copy-start | bytes 49156
  14.9 1.1 %copy-start.2 = (f32[1,2,128,640]{3,2,1,0:T(8,128)S(1)}, f32[1,2,128,640]{3,2,1,0:T(8,128)}, u32[]{:S(2)}) copy-start(f32[1,2,128,640]{3,2,1,0:T(8,128)} %refs_0_.3) | copy-start | bytes 1966084
  16.0 35.3 %copy-start.3 = (f32[1,2,128,640]{3,2,1,0:T(8,128)S(1)}, f32[1,2,128,640]{3,2,1,0:T(8,128)}, u32[]{:S(2)}) copy-start(f32[1,2,128,640]{3,2,1,0:T(8,128)} %refs_0_.3) | copy-start | bytes 1966084
  16.6 34.8 %copy-start.1 = (bf16[1,2,128,640]{3,2,1,0:T(8,128)(2,1)S(1)}, bf16[1,2,128,640]{3,2,1,0:T(8,128)(2,1)}, u32[]{:S(2)}) copy-start(bf16[1,2,128,640]{3,2,1,0:T(8,128)(2,1)} %refs_1_.3) | copy-start | bytes 983044

commit v2 on v0

v2 whole, which is shorter than its diff:
```python
import math

import jax
import jax.numpy as jnp
from jax import lax
from jax.experimental import pallas as pl
from jax.experimental.pallas import tpu as pltpu
from jax.sharding import Mesh, PartitionSpec as P

GROUP = 64
LANES = 128
decay_rate = 0.999
epsilon = 1e-06
f32 = jnp.float32
bf16 = jnp.bfloat16
SHIFT = 256.0


def kept_cosines(freq, place):
    turn = ((2 * place + 1) * freq) & 255
    turn = jnp.where(turn > 128, 256 - turn, turn)
    far = turn > 64
    angle = jnp.where(far, 128 - turn, turn).astype(f32) * (math.pi / 128)
    square = angle * angle
    series = jnp.full_like(square, 1 / math.factorial(12))
    for n in (10, 8, 6, 4, 2, 0):
        series = series * square + (1 if n % 4 == 0 else -1) / math.factorial(n)
    scale = jnp.where(freq == 0, math.sqrt(1.0 / GROUP), math.sqrt(2.0 / GROUP))
    return jnp.where(far, -series, series) * scale


def halves(x):
    high = x.astype(bf16)
    return high, (x - high.astype(f32)).astype(bf16)


def dot(a, b, transposed=False):
    dims = (((1,), (1 if transposed else 0,)), ((), ()))
    return lax.dot_general(a, b, dims, preferred_element_type=f32)


def times(x, b_high, b_low, transposed=False):
    x_high, x_low = halves(x)
    return dot(x_high, b_high, transposed) + (dot(x_high, b_low, transposed) + dot(x_low, b_high, transposed))


def block(ref, b):
    lanes = slice(b * LANES, (b + 1) * LANES)
    return jnp.concatenate([ref[0, layer, :, lanes] for layer in range(ref.shape[1])], axis=0)


def squares_kernel(grad_ref, squares_ref):
    layers = grad_ref.shape[1]
    totals = []
    for layer in range(layers):
        wide = grad_ref[0, layer].astype(f32)
        parts = jnp.sum((wide * wide).reshape(-1, 8, wide.shape[1]), axis=0)
        total = parts[:, 0:LANES]
        for b in range(1, wide.shape[1] // LANES):
            total = total + parts[:, b * LANES : (b + 1) * LANES]
        totals.append(total[0:4] + total[4:8])
    squares_ref[...] = jnp.broadcast_to(jnp.concatenate(totals, axis=0)[None], squares_ref.shape)


def code_kernel(mom_ref, grad_ref, kept_ref, coded_ref, pick_ref, high_ref, low_ref):
    kept = kept_ref[...]
    kept = jnp.concatenate([kept, kept], axis=1)
    place = lax.broadcasted_iota(jnp.int32, (GROUP, LANES), 0)
    lane = lax.broadcasted_iota(jnp.int32, (GROUP, LANES), 1)
    pick = kept_cosines(kept >> 6, place)
    cols = kept_cosines(kept & 63, place) * (1 / SHIFT)
    both = jnp.concatenate([jnp.where(lane < GROUP, cols, 0.0), jnp.where(lane < GROUP, 0.0, cols)], axis=0)
    high, low = halves(both)
    pick_ref[...] = pick * (SHIFT * SHIFT)
    high_ref[...] = high
    low_ref[...] = low

    def gathered(t):
        return jnp.sum(t.reshape(-1, GROUP, LANES) * pick[None], axis=1)

    for b in range(grad_ref.shape[3] // LANES):
        lanes = slice(b * LANES, (b + 1) * LANES)
        g = block(grad_ref, b)
        coded_ref[4:8, lanes] = gathered(dot(g, high) + dot(g, low))
        coded_ref[0:4, lanes] = gathered(times(block(mom_ref, b), high, low))


def spectra_kernel(count, squares_ref, coded_ref, own_ref, clip_ref, pair_ref):
    clips = []
    members = squares_ref.shape[0] // 2
    for core in range(2):
        total = jnp.sum(squares_ref[core * members : (core + 1) * members], axis=0)
        squares = [jnp.sum(total[i : i + 4], keepdims=True) for i in (0, 4)]
        square = jnp.concatenate([jnp.broadcast_to(s, (4, LANES)) for s in squares], axis=0)
        clips.append(1.0 / jnp.maximum(1.0, jnp.sqrt(square / count + epsilon)))
        clip_ref[core] = clips[core]
    for b in range(coded_ref.shape[2] // LANES):
        lanes = slice(b * LANES, (b + 1) * LANES)
        both = []
        for core in range(2):
            both.append(decay_rate * coded_ref[core, 0:4, lanes] + clips[core][2:6] * coded_ref[core, 4:8, lanes])
            own_ref[core, :, lanes] = both[core]
        pair_ref[:, lanes] = both[0] + both[1]


def decode_block(spectra, pick, b_high, b_low):
    wide = (spectra[:, None, :] * pick[None]).reshape(-1, LANES)
    return times(wide, b_high, b_low, True)


def momentum_kernel(mom_ref, grad_ref, clip_ref, own_ref, pick_ref, high_ref, low_ref, new_ref):
    layers, rows = grad_ref.shape[1:3]
    for b in range(grad_ref.shape[3] // LANES):
        lanes = slice(b * LANES, (b + 1) * LANES)
        own = decode_block(own_ref[:, lanes], pick_ref[...], high_ref[...], low_ref[...])
        for layer in range(layers):
            each = clip_ref[4 * layer : 4 * layer + 1, :]
            x = decay_rate * mom_ref[0, layer, :, lanes] + each * grad_ref[0, layer, :, lanes].astype(f32)
            new_ref[0, layer, :, lanes] = x - own[layer * rows : (layer + 1) * rows]


def update_kernel(total_ref, pick_ref, high_ref, low_ref, update_ref):
    layers, rows, cols = update_ref.shape
    lane = lax.broadcasted_iota(jnp.int32, (4, LANES), 1)
    for b in range(cols // LANES):
        lanes = slice(b * LANES, (b + 1) * LANES)
        tiles = decode_block(total_ref[:, lanes], pick_ref[...], high_ref[...], low_ref[...]).reshape(4, GROUP, LANES)
        size = jnp.sum(jnp.abs(tiles), axis=1)
        left = jnp.sum(jnp.where(lane < GROUP, size, 0.0), axis=1, keepdims=True)
        right = jnp.sum(jnp.where(lane < GROUP, 0.0, size), axis=1, keepdims=True)
        mean = jnp.where(lane < GROUP, left, right) / (GROUP * GROUP)
        scale = 1.0 / (mean + epsilon)
        update_ref[:, :, lanes] = jnp.tanh(tiles * scale[:, None, :]).astype(bf16).reshape(layers, rows, LANES)


def exchange(x, axes):
    return lax.all_to_all(x, axes, 0, 0, tiled=True)


def solution(mesh):
    whole = Mesh(mesh.devices.reshape(8, 4, 2, 2, 4), ("z", "yh", "core", "yl", "x"))
    rep, mp = ("z", "yh", "core"), ("yl", "x")

    def per_device(momentum, gradient, kept_index):
        _, layers, rows, cols = momentum.shape
        count = float(rows * cols * 8)
        sds = jax.ShapeDtypeStruct

        def call(kernel, name, cost, *outs):
            return pl.pallas_call(
                kernel,
                out_shape=outs if len(outs) > 1 else outs[0],
                compiler_params=pltpu.CompilerParams(vmem_limit_bytes=24 * 1024 * 1024),
                cost_estimate=pl.CostEstimate(flops=cost, bytes_accessed=2 * momentum.size * 4, transcendentals=0),
                name=name,
            )

        squares = call(squares_kernel, "squares", 1 << 20, sds((16, 8, LANES), f32))(gradient)
        squares = exchange(squares, ("core",) + mp)
        coded, pick, high, low = call(
            code_kernel, "transforms", 1 << 28,
            sds((8, cols), f32), sds((GROUP, LANES), f32), sds((LANES, LANES), bf16), sds((LANES, LANES), bf16),
        )(momentum, gradient, kept_index.reshape(1, GROUP))
        coded = lax.all_gather(coded, "core")
        own, clip, pair = call(
            lambda *refs: spectra_kernel(count, *refs), "spectra", 1 << 20,
            sds((2, 4, cols), f32), sds((2, 8, LANES), f32), sds((4, cols), f32),
        )(squares, coded)
        core = lax.axis_index("core")
        part = lax.dynamic_slice_in_dim(pair, 2 * core, 2)
        got = exchange(jnp.broadcast_to(part[None], (32, 2, cols)), ("z", "yh"))
        own = lax.dynamic_index_in_dim(own, core, keepdims=False)
        clip = lax.dynamic_index_in_dim(clip, core, keepdims=False)
        new = call(momentum_kernel, "new_momentum", 1 << 28, sds(momentum.shape, f32))(
            momentum, gradient, clip, own, pick, high, low
        )
        total = lax.all_gather(jnp.sum(got, axis=0), "core", tiled=True)
        update = call(update_kernel, "update", 1 << 28, sds((layers, rows, cols), bf16))(total, pick, high, low)
        return new, update

    return jax.shard_map(
        per_device,
        mesh=whole,
        in_specs=(P(rep, None, None, mp), P(rep, None, None, mp), P()),
        out_specs=(P(rep, None, None, mp), P(None, None, mp)),
        check_vma=False,
    )
```

time: 596 us -> 47.3 us (0.08)
  blocking collectives: 572 us -> 5.38 us
  starting transfers between devices: 0 us -> 21.6 us
  waiting for transfers between devices: 0 us -> 11.6 us
    unnamed x2 -> x0, blocking collectives: 555 us -> none
    all_to_all x0 -> x2, starting transfers between devices: none -> 21.6 us  [exchange(): return lax.all_to_all(x, axes, 0, 0, tiled=True)]
    psum x1 -> x0, blocking collectives: 16.8 us -> none  [per_device(): sum_squares = lax.psum(squares, 'mp')]
    all_to_all x0 -> x2, waiting for transfers between devices: none -> 11.6 us  [exchange(): return lax.all_to_all(x, axes, 0, 0, tiled=True)]
  transfers between devices with their start and end apart: 0 -> 2, of which waited for: 0 -> 2; matrix products, arithmetic and copies ran while one was open for 0% -> 0% of each run, Pallas kernels for 0% -> 4%
where the time goes in v2:
time: 47.3 us; the launch traced here: 47 us
  starting transfers between devices  21.6 us (46%)
  waiting for transfers between devices  11.6 us (25%)
  blocking collectives  5.38 us (11%)
  Pallas kernels  4.11 us (9%)
  local copies, waits for them, and re-layouts  3.46 us (7%)
  between operations  0.71 us (2%)
    all_to_all x2, starting transfers between devices, exchange(): return lax.all_to_all(x, axes, 0, 0, tiled=True)  21.6 us
    all_to_all x2, waiting for transfers between devices, exchange(): return lax.all_to_all(x, axes, 0, 0, tiled=True)  11.6 us
    all_gather x1, blocking collectives, per_device(): total = lax.all_gather(jnp.sum(got, axis=0), 'core', tiled=True)  3.55 us
    unnamed x11, local copies, waits for them, and re-layouts  2.72 us
    all_gather x1, blocking collectives, per_device(): coded = lax.all_gather(coded, 'core')  1.83 us
    pallas_call x1, Pallas kernels, per_device(): call(update_kernel, 'update', 1 << 28, sds((layers, rows, cols), bf16))  1.3 us
    pallas_call x1, Pallas kernels, per_device(): call(momentum_kernel, 'new_momentum', 1 << 28, sds(momentum.shape, f32))  1.27 us
  transfers between devices with their start and end apart: 2, of which 2 were waited for; matrix products, arithmetic and copies ran while one was open for 0% of the time, Pallas kernels for 4%

profile of v2, /device:TPU:1, one launch (start us, length us, event | category | flops | bytes accessed | tf_op | source)
XLA Modules:
  0.0 47.0 jit_solution(4384347809395794534)
XLA Ops:
  0.6 0.0 copy-start
  0.6 1.0 %copy-done = bf16[1,2,128,640]{3,2,1,0:T(8,128)(2,1)S(1)} copy-done((bf16[1,2,128,640]{3,2,1,0:T(8,128)(2,1)S(1)}, bf16[1,2,128,640]{3,2,1,0:T(8,128)(2,1)}, u32[]{:S(2)}) %copy-start) | copy-done | bytes 327704
  1.6 0.0 copy-start.1
  1.6 0.7 %squares.1 = f32[16,8,128]{2,1,0:T(8,128)} custom-call(bf16[1,2,128,640]{3,2,1,0:T(8,128)(2,1)S(1)} %copy-done), custom_call_target="tpu_custom_call" | custom-call | flops 1048576 | bytes 1310720 | tf_op jit(solution)/shard_map/squares/pallas_call | solution.py:158
  2.3 10.2 %all-to-all-start = ((f32[16,8,128]{2,1,0:T(8,128)}), f32[16,8,128]{2,1,0:T(8,128)S(1)}, u32[]{:S(2)}, u32[]{:S(2)}) async-start(f32[16,8,128]{2,1,0:T(8,128)} %squares.1), calls=%async_computation | async-start | bytes 131072 | tf_op jit(solution)/shard_map/all_to_all | solution.py:137
  12.5 0.0 copy-start.4
  12.5 0.0 copy-done.1
  12.5 0.6 %copy-done.4 = s32[64]{0:T(128)S(1)} copy-done((s32[64]{0:T(128)S(1)}, s32[64]{0:T(128)}, u32[]{:S(2)}) %copy-start.4) | copy-done | bytes 280
  13.2 0.0 copy-start.2
  13.2 1.1 %copy-done.2 = f32[1,2,128,640]{3,2,1,0:T(8,128)S(1)} copy-done((f32[1,2,128,640]{3,2,1,0:T(8,128)S(1)}, f32[1,2,128,640]{3,2,1,0:T(8,128)}, u32[]{:S(2)}) %copy-start.2) | copy-done | bytes 655384
  14.2 0.0 copy-start.3
  14.2 0.7 %transforms.1 = (f32[8,640]{1,0:T(8,128)S(1)}, f32[64,128]{1,0:T(8,128)S(1)}, bf16[128,128]{1,0:T(8,128)(2,1)S(1)}, bf16[128,128]{1,0:T(8,128)(2,1)S(1)}) custom-call(f32[1,2,128,640]{3,2,1,0:T(8,128)S(1)} %copy-done.2, bf16[1,2,128,640]{3,2,1,0:T(8,128)(2,1)S(1)} %copy-done.1, s32[1,64]{1,0:T(1,128)S(1)} %bitcast.8), custom_call_target="tpu_custom_call" | custom-call | flops 268435456 | bytes 1310720 | tf_op jit(solution)/shard_map/transforms/pallas_call | solution.py:160
  15.0 1.8 %all-gather = f32[16,640]{1,0:T(8,128)S(1)} all-gather(f32[8,640]{1,0:T(8,128)S(1)} %get-tuple-element.9), channel_id=2, replica_groups=mesh['z'=8,'yh'=4,'core'=2,'yl'=2,'x'=4] {'core'}, dimensions={0}, use_global_device_ids=true | all-gather | bytes 61440 | tf_op jit(solution)/shard_map/all_gather | solution.py:164
  16.8 1.5 %all-to-all-done.refs_0_ = f32[16,8,128]{2,1,0:T(8,128)S(1)} async-done(((f32[16,8,128]{2,1,0:T(8,128)}), f32[16,8,128]{2,1,0:T(8,128)S(1)}, u32[]{:S(2)}, u32[]{:S(2)}) %all-to-all-start) | async-done | bytes 65568 | tf_op jit(solution)/shard_map/all_to_all | solution.py:137
  18.3 0.1 spectra.1
  18.5 0.7 %broadcast_in_dim.2 = f32[32,2,640]{2,1,0:T(2,128)} broadcast(f32[2,640]{1,0:T(2,128)S(1)} %constant_dynamic-slice_fusion), dimensions={1,2} | broadcast | bytes 168960 | tf_op jit(solution)/shard_map/broadcast_in_dim | solution.py:171
  19.2 11.4 %all-to-all-start.1 = ((f32[32,2,640]{2,1,0:T(2,128)}), f32[32,2,640]{2,1,0:T(2,128)S(1)}, u32[]{:S(2)}, u32[]{:S(2)}) async-start(f32[32,2,640]{2,1,0:T(2,128)} %broadcast_in_dim.2), calls=%async_computation.1 | async-start | bytes 327680 | tf_op jit(solution)/shard_map/all_to_all | solution.py:137
  30.7 0.0 copy-done.3
  30.7 1.3 %new_momentum.1 = f32[1,2,128,640]{3,2,1,0:T(8,128)} custom-call(f32[1,2,128,640]{3,2,1,0:T(8,128)S(1)} %copy-done.3, bf16[1,2,128,640]{3,2,1,0:T(8,128)(2,1)S(1)} %copy-done.1, f32[8,128]{1,0:T(8,128)S(1)} %dynamic-slice_bitcast_fusion.1.clip_ref, f32[4,640]{1,0:T(4,128)S(1)} %dynamic-slice_bitcast_fusion.own_ref, ...), custom_call_target="tpu_custom_call" | custom-call | flops 268435456 | bytes 1310720 | tf_op jit(solution)/shard_map/new_momentum/pallas_call | solution.py:174
  32.0 10.1 %all-to-all-done.1 = f32[32,2,640]{2,1,0:T(2,128)S(1)} async-done(((f32[32,2,640]{2,1,0:T(2,128)}), f32[32,2,640]{2,1,0:T(2,128)S(1)}, u32[]{:S(2)}, u32[]{:S(2)}) %all-to-all-start.1) | async-done | bytes 163872 | tf_op jit(solution)/shard_map/all_to_all | solution.py:137
  42.0 0.1 reduce_sum.9
  42.1 3.5 %all-gather.1 = f32[2,2,640]{2,1,0:T(2,128)S(1)} all-gather(f32[1,2,640]{2,1,0:T(2,128)S(1)} %bitcast.9), channel_id=1, replica_groups=mesh['z'=8,'yh'=4,'core'=2,'yl'=2,'x'=4] {'core'}, dimensions={0}, use_global_device_ids=true | all-gather | bytes 15360 | tf_op jit(solution)/shard_map/all_gather | solution.py:177
  45.7 1.3 %update.1 = bf16[2,128,640]{2,1,0:T(8,128)(2,1)} custom-call(f32[4,640]{1,0:T(4,128)S(1)} %reshape.11.total_ref, f32[64,128]{1,0:T(8,128)S(1)} %get-tuple-element.12.pick_ref, bf16[128,128]{1,0:T(8,128)(2,1)S(1)} %get-tuple-element.13.high_ref, bf16[128,128]{1,0:T(8,128)(2,1)S(1)} %get-tuple-element.14.low_ref), custom_call_target="tpu_custom_call" | custom-call | flops 268435456 | bytes 1310720 | tf_op jit(solution)/shard_map/update/pallas_call | solution.py:178
  (4 shorter events, 0.0 us)
Async XLA Ops:
  0.6 1.0 %copy-start = (bf16[1,2,128,640]{3,2,1,0:T(8,128)(2,1)S(1)}, bf16[1,2,128,640]{3,2,1,0:T(8,128)(2,1)}, u32[]{:S(2)}) copy-start(bf16[1,2,128,640]{3,2,1,0:T(8,128)(2,1)} %grad_ref.5) | copy-start | bytes 983044
  1.6 10.9 %copy-start.1 = (bf16[1,2,128,640]{3,2,1,0:T(8,128)(2,1)S(1)}, bf16[1,2,128,640]{3,2,1,0:T(8,128)(2,1)}, u32[]{:S(2)}) copy-start(bf16[1,2,128,640]{3,2,1,0:T(8,128)(2,1)} %grad_ref.5) | copy-start | bytes 983044
  2.3 16.1 %all-to-all-start = ((f32[16,8,128]{2,1,0:T(8,128)}), f32[16,8,128]{2,1,0:T(8,128)S(1)}, u32[]{:S(2)}, u32[]{:S(2)}) async-start(f32[16,8,128]{2,1,0:T(8,128)} %squares.1), calls=%async_computation | async-start | bytes 131072 | tf_op jit(solution)/shard_map/all_to_all | solution.py:137
  12.5 0.7 %copy-start.4 = (s32[64]{0:T(128)S(1)}, s32[64]{0:T(128)}, u32[]{:S(2)}) copy-start(s32[64]{0:T(128)} %param.5) | copy-start | bytes 772
  13.2 1.1 %copy-start.2 = (f32[1,2,128,640]{3,2,1,0:T(8,128)S(1)}, f32[1,2,128,640]{3,2,1,0:T(8,128)}, u32[]{:S(2)}) copy-start(f32[1,2,128,640]{3,2,1,0:T(8,128)} %mom_ref.3) | copy-start | bytes 1966084
  14.2 16.5 %copy-start.3 = (f32[1,2,128,640]{3,2,1,0:T(8,128)S(1)}, f32[1,2,128,640]{3,2,1,0:T(8,128)}, u32[]{:S(2)}) copy-start(f32[1,2,128,640]{3,2,1,0:T(8,128)} %mom_ref.3) | copy-start | bytes 1966084
  19.2 22.8 %all-to-all-start.1 = ((f32[32,2,640]{2,1,0:T(2,128)}), f32[32,2,640]{2,1,0:T(2,128)S(1)}, u32[]{:S(2)}, u32[]{:S(2)}) async-start(f32[32,2,640]{2,1,0:T(2,128)} %broadcast_in_dim.2), calls=%async_computation.1 | async-start | bytes 327680 | tf_op jit(solution)/shard_map/all_to_all | solution.py:137

commit v3 on v2

v3 whole, which is shorter than its diff:
```python
import math

import jax
import jax.numpy as jnp
from jax import lax
from jax.experimental import pallas as pl
from jax.experimental.pallas import tpu as pltpu
from jax.sharding import Mesh, PartitionSpec as P

GROUP = 64
LANES = 128
decay_rate = 0.999
epsilon = 1e-06
f32 = jnp.float32
bf16 = jnp.bfloat16
SHIFT = 256.0


def kept_cosines(freq, place):
    turn = ((2 * place + 1) * freq) & 255
    turn = jnp.where(turn > 128, 256 - turn, turn)
    far = turn > 64
    angle = jnp.where(far, 128 - turn, turn).astype(f32) * (math.pi / 128)
    square = angle * angle
    series = jnp.full_like(square, 1 / math.factorial(12))
    for n in (10, 8, 6, 4, 2, 0):
        series = series * square + (1 if n % 4 == 0 else -1) / math.factorial(n)
    scale = jnp.where(freq == 0, math.sqrt(1.0 / GROUP), math.sqrt(2.0 / GROUP))
    return jnp.where(far, -series, series) * scale


def halves(x):
    high = x.astype(bf16)
    return high, (x - high.astype(f32)).astype(bf16)


def dot(a, b, transposed=False):
    dims = (((1,), (1 if transposed else 0,)), ((), ()))
    return lax.dot_general(a, b, dims, preferred_element_type=f32)


def times(x, wide, transposed=False):
    both = dot(jnp.concatenate(halves(x), axis=1), wide, transposed)
    return both[:, 0:LANES] + both[:, LANES : 2 * LANES]


def joined(high, low, transposed=False):
    zero = jnp.zeros_like(low)
    across, down = ((high, high), (low, zero)) if transposed else ((high, low), (high, zero))
    return jnp.concatenate([jnp.concatenate(across, axis=1), jnp.concatenate(down, axis=1)], axis=0)


def block(ref, b):
    lanes = slice(b * LANES, (b + 1) * LANES)
    return jnp.concatenate([ref[0, layer, :, lanes] for layer in range(ref.shape[1])], axis=0)


def first_kernel(mom_hbm, grad_hbm, kept_hbm, squares_hbm, mom_ref, grad_ref, pick_ref, code_ref, decode_ref, squares_ref, kept_ref, sems):
    layers = grad_ref.shape[1]
    copies = [pltpu.make_async_copy(grad_hbm.at[:, i], grad_ref.at[:, i], sems.at[i]) for i in range(layers)]
    copies += [pltpu.make_async_copy(kept_hbm, kept_ref, sems.at[layers])]
    copies += [pltpu.make_async_copy(mom_hbm, mom_ref, sems.at[layers + 1])]
    for copy in copies:
        copy.start()

    copies[layers].wait()
    kept = kept_ref[...]
    kept = jnp.concatenate([kept, kept], axis=1)
    place = lax.broadcasted_iota(jnp.int32, (GROUP, LANES), 0)
    lane = lax.broadcasted_iota(jnp.int32, (GROUP, LANES), 1)
    pick_ref[...] = kept_cosines(kept >> 6, place) * (SHIFT * SHIFT)
    cols = kept_cosines(kept & 63, place) * (1 / SHIFT)
    both = jnp.concatenate([jnp.where(lane < GROUP, cols, 0.0), jnp.where(lane < GROUP, 0.0, cols)], axis=0)
    high, low = halves(both)
    code_ref[...] = joined(high, low)
    decode_ref[...] = joined(high, low, transposed=True)

    for layer in range(layers):
        copies[layer].wait()
        wide = grad_ref[0, layer].astype(f32)
        parts = jnp.sum((wide * wide).reshape(-1, 8, wide.shape[1]), axis=0)
        total = parts[:, 0:LANES]
        for b in range(1, wide.shape[1] // LANES):
            total = total + parts[:, b * LANES : (b + 1) * LANES]
        total = total[0:4] + total[4:8]
        squares_ref[:, 4 * layer : 4 * layer + 4] = jnp.broadcast_to(total[None], (squares_ref.shape[0], 4, LANES))
    out = pltpu.make_async_copy(squares_ref, squares_hbm, sems.at[layers + 2])
    out.start()
    copies[-1].wait()
    out.wait()


def code_kernel(mom_ref, grad_ref, pick_ref, code_ref, coded_ref):
    pick = pick_ref[...] * (1 / (SHIFT * SHIFT))
    code = code_ref[...]

    def gathered(t):
        return jnp.sum(t.reshape(-1, GROUP, LANES) * pick[None], axis=1)

    for b in range(grad_ref.shape[3] // LANES):
        lanes = slice(b * LANES, (b + 1) * LANES)
        g = dot(block(grad_ref, b), code[0:LANES])
        coded_ref[4:8, lanes] = gathered(g[:, 0:LANES] + g[:, LANES : 2 * LANES])
        coded_ref[0:4, lanes] = gathered(times(block(mom_ref, b), code))


def spectra_kernel(count, squares_ref, coded_ref, copies_hbm, own_ref, clip_ref, copies_ref, sems):
    here = lax.axis_index("core")
    clips = []
    members = squares_ref.shape[0] // 2
    for core in range(2):
        total = jnp.sum(squares_ref[core * members : (core + 1) * members], axis=0)
        squares = [jnp.sum(total[i : i + 4], keepdims=True) for i in (0, 4)]
        square = jnp.concatenate([jnp.broadcast_to(s, (4, LANES)) for s in squares], axis=0)
        clips.append(1.0 / jnp.maximum(1.0, jnp.sqrt(square / count + epsilon)))
    clip_ref[...] = jnp.where(here == 0, clips[0], clips[1])
    for b in range(coded_ref.shape[2] // LANES):
        lanes = slice(b * LANES, (b + 1) * LANES)
        both = [decay_rate * coded_ref[core, 0:4, lanes] + clips[core][2:6] * coded_ref[core, 4:8, lanes] for core in range(2)]
        own_ref[:, lanes] = jnp.where(here == 0, both[0], both[1])
        pair = both[0] + both[1]
        part = jnp.where(here == 0, pair[0:2], pair[2:4])
        copies_ref[:, :, lanes] = jnp.broadcast_to(part[None], (copies_ref.shape[0], 2, LANES))
    size = copies_ref.shape[0]
    out = [pltpu.make_async_copy(copies_ref, copies_hbm.at[pl.ds(i * size, size)], sems.at[i]) for i in range(copies_hbm.shape[0] // size)]
    for copy in out:
        copy.start()
    for copy in out:
        copy.wait()


def decode_block(spectra, pick, decode):
    return times((spectra[:, None, :] * pick[None]).reshape(-1, LANES), decode, transposed=True)


def momentum_kernel(mom_ref, grad_ref, clip_ref, own_ref, pick_ref, decode_ref, new_ref):
    layers, rows = grad_ref.shape[1:3]
    for b in range(grad_ref.shape[3] // LANES):
        lanes = slice(b * LANES, (b + 1) * LANES)
        own = decode_block(own_ref[:, lanes], pick_ref[...], decode_ref[...])
        for layer in range(layers):
            each = clip_ref[4 * layer : 4 * layer + 1, :]
            x = decay_rate * mom_ref[0, layer, :, lanes] + each * grad_ref[0, layer, :, lanes].astype(f32)
            new_ref[0, layer, :, lanes] = x - own[layer * rows : (layer + 1) * rows]


def update_kernel(total_ref, pick_ref, decode_ref, update_hbm, update_ref, sems):
    layers, rows, cols = update_ref.shape
    lane = lax.broadcasted_iota(jnp.int32, (4, LANES), 1)
    copies = []
    for b in range(cols // LANES):
        lanes = slice(b * LANES, (b + 1) * LANES)
        tiles = decode_block(total_ref[:, lanes], pick_ref[...], decode_ref[...]).reshape(4, GROUP, LANES)
        size = jnp.sum(jnp.abs(tiles), axis=1)
        left = jnp.sum(jnp.where(lane < GROUP, size, 0.0), axis=1, keepdims=True)
        right = jnp.sum(jnp.where(lane < GROUP, 0.0, size), axis=1, keepdims=True)
        mean = jnp.where(lane < GROUP, left, right) / (GROUP * GROUP)
        scale = 1.0 / (mean + epsilon)
        update_ref[:, :, lanes] = jnp.tanh(tiles * scale[:, None, :]).astype(bf16).reshape(layers, rows, LANES)
        part = pl.ds(b * LANES, LANES)
        copies.append(pltpu.make_async_copy(update_ref.at[:, :, part], update_hbm.at[:, :, part], sems.at[b]))
        copies[b].start()
    for copy in copies:
        copy.wait()


def exchange(x, axes):
    return lax.all_to_all(x, axes, 0, 0, tiled=True)


def solution(mesh):
    whole = Mesh(mesh.devices.reshape(8, 4, 2, 2, 4), ("z", "yh", "core", "yl", "x"))
    rep, mp = ("z", "yh", "core"), ("yl", "x")

    def per_device(momentum, gradient, kept_index):
        _, layers, rows, cols = momentum.shape
        count = float(rows * cols * 8)
        sds = jax.ShapeDtypeStruct

        def call(kernel, name, cost, *outs):
            return pl.pallas_call(
                kernel,
                out_shape=outs if len(outs) > 1 else outs[0],
                compiler_params=pltpu.CompilerParams(vmem_limit_bytes=24 * 1024 * 1024),
                cost_estimate=pl.CostEstimate(flops=cost, bytes_accessed=2 * momentum.size * 4, transcendentals=0),
                name=name,
            )

        shapes = (momentum.shape, f32), (gradient.shape, bf16), ((GROUP, LANES), f32), ((2 * LANES, 2 * LANES), bf16), ((2 * LANES, 2 * LANES), bf16)
        hbm = lambda x: pltpu.with_memory_space_constraint(x, pltpu.HBM)
        squares, momentum, gradient, pick, code, decode = pl.pallas_call(
            first_kernel,
            in_specs=[pl.BlockSpec(memory_space=pltpu.HBM)] * 3,
            out_shape=(pltpu.HBM((16, 8, LANES), f32), *[pltpu.VMEM(*s) for s in shapes]),
            out_specs=(pl.BlockSpec(memory_space=pltpu.HBM),) + (pl.BlockSpec(memory_space=pltpu.VMEM),) * 5,
            scratch_shapes=[
                pltpu.VMEM((16, 8, LANES), f32),
                pltpu.VMEM((1, GROUP), jnp.int32),
                pltpu.SemaphoreType.DMA((layers + 3,)),
            ],
            compiler_params=pltpu.CompilerParams(vmem_limit_bytes=24 * 1024 * 1024),
            name="squares",
        )(hbm(momentum), hbm(gradient), hbm(kept_index.reshape(1, GROUP)))
        squares = exchange(squares, ("core",) + mp)
        coded = call(code_kernel, "transforms", 1 << 28, sds((8, cols), f32))(momentum, gradient, pick, code)
        coded = lax.all_gather(coded, "core")
        copies, own, clip = pl.pallas_call(
            lambda *refs: spectra_kernel(count, *refs),
            out_shape=(pltpu.HBM((32, 2, cols), f32), pltpu.VMEM((4, cols), f32), pltpu.VMEM((8, LANES), f32)),
            out_specs=(pl.BlockSpec(memory_space=pltpu.HBM),) + (pl.BlockSpec(memory_space=pltpu.VMEM),) * 2,
            scratch_shapes=[pltpu.VMEM((8, 2, cols), f32), pltpu.SemaphoreType.DMA((4,))],
            compiler_params=pltpu.CompilerParams(vmem_limit_bytes=24 * 1024 * 1024),
            name="spectra",
        )(squares, coded)
        got = exchange(copies, ("z", "yh"))
        new = call(momentum_kernel, "new_momentum", 1 << 28, sds(momentum.shape, f32))(
            momentum, gradient, clip, own, pick, decode
        )
        total = lax.all_gather(jnp.sum(got, axis=0), "core", tiled=True)
        update = pl.pallas_call(
            update_kernel,
            out_shape=pltpu.HBM((layers, rows, cols), bf16),
            out_specs=pl.BlockSpec(memory_space=pltpu.HBM),
            scratch_shapes=[pltpu.VMEM((layers, rows, cols), bf16), pltpu.SemaphoreType.DMA((cols // LANES,))],
            compiler_params=pltpu.CompilerParams(vmem_limit_bytes=24 * 1024 * 1024),
            name="update",
        )(total, pick, decode)
        return new, update

    return jax.shard_map(
        per_device,
        mesh=whole,
        in_specs=(P(rep, None, None, mp), P(rep, None, None, mp), P()),
        out_specs=(P(rep, None, None, mp), P(None, None, mp)),
        check_vma=False,
    )
```

time: 47.3 us -> 47.2 us (level)
  local copies, waits for them, and re-layouts: 3.46 us -> 0.02 us
  waiting for transfers between devices: 11.6 us -> 13.7 us
  Pallas kernels: 4.11 us -> 5.47 us
    unnamed x11 -> x1, local copies, waits for them, and re-layouts: 2.72 us -> 0.02 us
    all_to_all x2, waiting for transfers between devices: 11.6 us -> 13.7 us  [exchange(): return lax.all_to_all(x, axes, 0, 0, tiled=True)]
    pallas_call x4, Pallas kernels: 2.84 us -> 4.25 us  [the longest x1 1.71 us: per_device(): pl.pallas_call(first_kernel, in_specs=[pl.BlockSpec(memory_space=pltpu.HB...]
    broadcast_in_dim x1 -> x0, local copies, waits for them, and re-layouts: 0.71 us -> none  [per_device(): got = exchange(jnp.broadcast_to(part[None], (32, 2, cols)), ('z', 'yh'))]
where the time goes in v3:
time: 47.2 us; the launch traced here: 46.9 us
  starting transfers between devices  21.7 us (46%)
  waiting for transfers between devices  13.7 us (29%)
  Pallas kernels  5.47 us (12%)
  blocking collectives  5.38 us (11%)
  between operations  0.66 us (1%)
    all_to_all x2, starting transfers between devices, exchange(): return lax.all_to_all(x, axes, 0, 0, tiled=True)  21.7 us
    all_to_all x2, waiting for transfers between devices, exchange(): return lax.all_to_all(x, axes, 0, 0, tiled=True)  13.7 us
    all_gather x1, blocking collectives, per_device(): total = lax.all_gather(jnp.sum(got, axis=0), 'core', tiled=True)  3.55 us
    all_gather x1, blocking collectives, per_device(): coded = lax.all_gather(coded, 'core')  1.83 us
    pallas_call x1, Pallas kernels, per_device(): pl.pallas_call(first_kernel, in_specs=[pl.BlockSpec(memory_space=pltpu.HB...  1.71 us
    pallas_call x1, Pallas kernels, per_device(): call(momentum_kernel, 'new_momentum', 1 << 28, sds(momentum.shape, f32))  1.22 us
    pallas_call x1, Pallas kernels, per_device(): pl.pallas_call(update_kernel, out_shape=pltpu.HBM((layers, rows, cols), b...  1.19 us
  transfers between devices with their start and end apart: 2, of which 2 were waited for; matrix products, arithmetic and copies ran while one was open for 0% of the time, Pallas kernels for 4%

profile of v3, /device:TPU:1, one launch (start us, length us, event | category | flops | bytes accessed | tf_op | source)
XLA Modules:
  0.0 46.9 jit_solution(1699339213442564115)
XLA Ops:
  0.6 1.7 %squares.1 = (f32[16,8,128]{2,1,0:T(8,128)}, f32[1,2,128,640]{3,2,1,0:T(8,128)S(1)}, bf16[1,2,128,640]{3,2,1,0:T(8,128)(2,1)S(1)}, f32[64,128]{1,0:T(8,128)S(1)}...) custom-call(f32[1,2,128,640]{3,2,1,0:T(8,128)} %mom_hbm.1, bf16[1,2,128,640]{3,2,1,0:T(8,128)(2,1)} %grad_hbm.1, ...), custom_call_target="tpu_custom_call" | custom-call | tf_op jit(solution)/shard_map/squares/pallas_call | solution.py:191
  2.3 10.2 %all-to-all-start = ((f32[16,8,128]{2,1,0:T(8,128)}), f32[16,8,128]{2,1,0:T(8,128)S(1)}, u32[]{:S(2)}, u32[]{:S(2)}) async-start(f32[16,8,128]{2,1,0:T(8,128)} %get-tuple-element.13), calls=%async_computation | async-start | bytes 131072 | tf_op jit(solution)/shard_map/all_to_all | solution.py:168
  12.6 0.5 %transforms.1 = f32[8,640]{1,0:T(8,128)S(1)} custom-call(f32[1,2,128,640]{3,2,1,0:T(8,128)S(1)} %get-tuple-element.11.mom_ref, bf16[1,2,128,640]{3,2,1,0:T(8,128)(2,1)S(1)} %get-tuple-element.12.grad_ref, f32[64,128]{1,0:T(8,128)S(1)} %get-tuple-element.14.pick_ref, bf16[256,256]{1,0:T(8,128)(2,1)S(1)} %get-tuple-element.15.code_ref), custom_call_target="tpu_custom_call" | custom-call | flops 268435456 | bytes 1310720 | tf_op jit(solution)/shard_map/transforms/pallas_call | solution.py:205
  13.1 1.8 %all-gather = f32[16,640]{1,0:T(8,128)S(1)} all-gather(f32[8,640]{1,0:T(8,128)S(1)} %transforms.1), channel_id=2, replica_groups=mesh['z'=8,'yh'=4,'core'=2,'yl'=2,'x'=4] {'core'}, dimensions={0}, use_global_device_ids=true | all-gather | bytes 61440 | tf_op jit(solution)/shard_map/all_gather | solution.py:206
  14.9 3.5 %all-to-all-done.refs_0_ = f32[16,8,128]{2,1,0:T(8,128)S(1)} async-done(((f32[16,8,128]{2,1,0:T(8,128)}), f32[16,8,128]{2,1,0:T(8,128)S(1)}, u32[]{:S(2)}, u32[]{:S(2)}) %all-to-all-start) | async-done | bytes 65568 | tf_op jit(solution)/shard_map/all_to_all | solution.py:168
  18.4 0.9 %spectra.1 = (f32[32,2,640]{2,1,0:T(2,128)}, f32[4,640]{1,0:T(4,128)S(1)}, f32[8,128]{1,0:T(8,128)S(1)}) custom-call(f32[16,8,128]{2,1,0:T(8,128)S(1)} %all-to-all-done.refs_0_, f32[2,8,640]{2,1,0:T(8,128)S(1)} %bitcast.3), custom_call_target="tpu_custom_call" | custom-call | tf_op jit(solution)/shard_map/spectra/pallas_call | solution.py:207
  19.3 11.4 %all-to-all-start.1 = ((f32[32,2,640]{2,1,0:T(2,128)}), f32[32,2,640]{2,1,0:T(2,128)S(1)}, u32[]{:S(2)}, u32[]{:S(2)}) async-start(f32[32,2,640]{2,1,0:T(2,128)} %get-tuple-element.19), calls=%async_computation.1 | async-start | bytes 327680 | tf_op jit(solution)/shard_map/all_to_all | solution.py:168
  30.7 1.2 %new_momentum.1 = f32[1,2,128,640]{3,2,1,0:T(8,128)} custom-call(f32[1,2,128,640]{3,2,1,0:T(8,128)S(1)} %get-tuple-element.11.mom_ref, bf16[1,2,128,640]{3,2,1,0:T(8,128)(2,1)S(1)} %get-tuple-element.12.grad_ref, f32[8,128]{1,0:T(8,128)S(1)} %get-tuple-element.16.clip_ref, f32[4,640]{1,0:T(4,128)S(1)} %get-tuple-element.17.own_ref, ...), custom_call_target="tpu_custom_call" | custom-call | flops 268435456 | bytes 1310720 | tf_op jit(solution)/shard_map/new_momentum/pallas_call | solution.py:216
  31.9 10.2 %all-to-all-done.1 = f32[32,2,640]{2,1,0:T(2,128)S(1)} async-done(((f32[32,2,640]{2,1,0:T(2,128)}), f32[32,2,640]{2,1,0:T(2,128)S(1)}, u32[]{:S(2)}, u32[]{:S(2)}) %all-to-all-start.1) | async-done | bytes 163872 | tf_op jit(solution)/shard_map/all_to_all | solution.py:168
  42.1 0.1 reduce_sum.9
  42.2 3.5 %all-gather.1 = f32[2,2,640]{2,1,0:T(2,128)S(1)} all-gather(f32[1,2,640]{2,1,0:T(2,128)S(1)} %bitcast.4), channel_id=1, replica_groups=mesh['z'=8,'yh'=4,'core'=2,'yl'=2,'x'=4] {'core'}, dimensions={0}, use_global_device_ids=true | all-gather | bytes 15360 | tf_op jit(solution)/shard_map/all_gather | solution.py:219
  45.7 1.2 %update.1 = bf16[2,128,640]{2,1,0:T(8,128)(2,1)} custom-call(f32[4,640]{1,0:T(4,128)S(1)} %reshape.10.total_ref, f32[64,128]{1,0:T(8,128)S(1)} %get-tuple-element.14.pick_ref, bf16[256,256]{1,0:T(8,128)(2,1)S(1)} %get-tuple-element.18.decode_ref), custom_call_target="tpu_custom_call" | custom-call | tf_op jit(solution)/shard_map/update/pallas_call | solution.py:220
  (1 shorter events, 0.0 us)
Async XLA Ops:
  2.3 16.1 %all-to-all-start = ((f32[16,8,128]{2,1,0:T(8,128)}), f32[16,8,128]{2,1,0:T(8,128)S(1)}, u32[]{:S(2)}, u32[]{:S(2)}) async-start(f32[16,8,128]{2,1,0:T(8,128)} %get-tuple-element.13), calls=%async_computation | async-start | bytes 131072 | tf_op jit(solution)/shard_map/all_to_all | solution.py:168
  19.3 22.8 %all-to-all-start.1 = ((f32[32,2,640]{2,1,0:T(2,128)}), f32[32,2,640]{2,1,0:T(2,128)S(1)}, u32[]{:S(2)}, u32[]{:S(2)}) async-start(f32[32,2,640]{2,1,0:T(2,128)} %get-tuple-element.19), calls=%async_computation.1 | async-start | bytes 327680 | tf_op jit(solution)/shard_map/all_to_all | solution.py:168

commit v4 on v3

--- a/solution.py
+++ b/solution.py
@@ -90,21 +90,32 @@
     out.wait()
 
 
-def code_kernel(mom_ref, grad_ref, pick_ref, code_ref, coded_ref):
-    pick = pick_ref[...] * (1 / (SHIFT * SHIFT))
-    code = code_ref[...]
+def code_kernel(mom_ref, grad_ref, pick_ref, code_ref, decode_ref, coded_ref, rest_mom_ref, rest_grad_ref):
+    layers, rows = grad_ref.shape[1:3]
+    wide_pick = pick_ref[...]
+    pick = wide_pick * (1 / (SHIFT * SHIFT))
+    code, decode = code_ref[...], decode_ref[...]
 
     def gathered(t):
         return jnp.sum(t.reshape(-1, GROUP, LANES) * pick[None], axis=1)
 
     for b in range(grad_ref.shape[3] // LANES):
         lanes = slice(b * LANES, (b + 1) * LANES)
-        g = dot(block(grad_ref, b), code[0:LANES])
-        coded_ref[4:8, lanes] = gathered(g[:, 0:LANES] + g[:, LANES : 2 * LANES])
-        coded_ref[0:4, lanes] = gathered(times(block(mom_ref, b), code))
-
-
-def spectra_kernel(count, squares_ref, coded_ref, copies_hbm, own_ref, clip_ref, copies_ref, sems):
+        g = block(grad_ref, b)
+        t = dot(g, code[0:LANES])
+        coded_grad = gathered(t[:, 0:LANES] + t[:, LANES : 2 * LANES])
+        m = block(mom_ref, b)
+        coded_mom = gathered(times(m, code))
+        coded_ref[4:8, lanes] = coded_grad
+        coded_ref[0:4, lanes] = coded_mom
+        rest_mom = decay_rate * (m - decode_block(coded_mom, wide_pick, decode))
+        rest_grad = g.astype(f32) * (1 / SHIFT) - decode_block(coded_grad, pick, decode) * SHIFT
+        for layer in range(layers):
+            rest_mom_ref[0, layer, :, lanes] = rest_mom[layer * rows : (layer + 1) * rows]
+            rest_grad_ref[0, layer, :, lanes] = rest_grad[layer * rows : (layer + 1) * rows]
+
+
+def spectra_kernel(count, squares_ref, coded_ref, copies_ref, clip_ref):
     here = lax.axis_index("core")
     clips = []
     members = squares_ref.shape[0] // 2
@@ -117,37 +128,26 @@
     for b in range(coded_ref.shape[2] // LANES):
         lanes = slice(b * LANES, (b + 1) * LANES)
         both = [decay_rate * coded_ref[core, 0:4, lanes] + clips[core][2:6] * coded_ref[core, 4:8, lanes] for core in range(2)]
-        own_ref[:, lanes] = jnp.where(here == 0, both[0], both[1])
         pair = both[0] + both[1]
         part = jnp.where(here == 0, pair[0:2], pair[2:4])
         copies_ref[:, :, lanes] = jnp.broadcast_to(part[None], (copies_ref.shape[0], 2, LANES))
-    size = copies_ref.shape[0]
-    out = [pltpu.make_async_copy(copies_ref, copies_hbm.at[pl.ds(i * size, size)], sems.at[i]) for i in range(copies_hbm.shape[0] // size)]
-    for copy in out:
-        copy.start()
-    for copy in out:
-        copy.wait()
 
 
 def decode_block(spectra, pick, decode):
     return times((spectra[:, None, :] * pick[None]).reshape(-1, LANES), decode, transposed=True)
 
 
-def momentum_kernel(mom_ref, grad_ref, clip_ref, own_ref, pick_ref, decode_ref, new_ref):
-    layers, rows = grad_ref.shape[1:3]
-    for b in range(grad_ref.shape[3] // LANES):
-        lanes = slice(b * LANES, (b + 1) * LANES)
-        own = decode_block(own_ref[:, lanes], pick_ref[...], decode_ref[...])
-        for layer in range(layers):
+def last_kernel(rest_mom_ref, rest_grad_ref, clip_ref, total_ref, pick_ref, decode_ref, new_hbm, update_hbm, new_ref, update_ref, sems):
+    layers, rows, cols = update_ref.shape
+    copies = []
+    for layer in range(layers):
+        for b in range(cols // LANES):
+            lanes = slice(b * LANES, (b + 1) * LANES)
             each = clip_ref[4 * layer : 4 * layer + 1, :]
-            x = decay_rate * mom_ref[0, layer, :, lanes] + each * grad_ref[0, layer, :, lanes].astype(f32)
-            new_ref[0, layer, :, lanes] = x - own[layer * rows : (layer + 1) * rows]
-
-
-def update_kernel(total_ref, pick_ref, decode_ref, update_hbm, update_ref, sems):
-    layers, rows, cols = update_ref.shape
+            new_ref[0, layer, :, lanes] = rest_mom_ref[0, layer, :, lanes] + (each * rest_grad_ref[0, layer, :, lanes]) * SHIFT
+        copies.append(pltpu.make_async_copy(new_ref.at[:, layer], new_hbm.at[:, layer], sems.at[layer]))
+        copies[-1].start()
     lane = lax.broadcasted_iota(jnp.int32, (4, LANES), 1)
-    copies = []
     for b in range(cols // LANES):
         lanes = slice(b * LANES, (b + 1) * LANES)
         tiles = decode_block(total_ref[:, lanes], pick_ref[...], decode_ref[...]).reshape(4, GROUP, LANES)
@@ -158,33 +158,29 @@
         scale = 1.0 / (mean + epsilon)
         update_ref[:, :, lanes] = jnp.tanh(tiles * scale[:, None, :]).astype(bf16).reshape(layers, rows, LANES)
         part = pl.ds(b * LANES, LANES)
-        copies.append(pltpu.make_async_copy(update_ref.at[:, :, part], update_hbm.at[:, :, part], sems.at[b]))
-        copies[b].start()
+        copies.append(pltpu.make_async_copy(update_ref.at[:, :, part], update_hbm.at[:, :, part], sems.at[layers + b]))
+        copies[-1].start()
     for copy in copies:
         copy.wait()
 
 
-def exchange(x, axes):
-    return lax.all_to_all(x, axes, 0, 0, tiled=True)
+def exchange(x, axes, groups):
+    return lax.all_to_all(x, axes, 0, 0, axis_index_groups=groups, tiled=True)
 
 
 def solution(mesh):
     whole = Mesh(mesh.devices.reshape(8, 4, 2, 2, 4), ("z", "yh", "core", "yl", "x"))
     rep, mp = ("z", "yh", "core"), ("yl", "x")
+
+    first_groups = [[core * 8 + (yl ^ 1) * 4 + (x + 2) % 4 for core in range(2) for yl in range(2) for x in range(4)]]
+    second_groups = [
+        [(((z + 6) % 8) * 4 + (yh + 2) % 4) * 2 + core for z in range(8) for yh in range(4)] for core in range(2)
+    ]
 
     def per_device(momentum, gradient, kept_index):
         _, layers, rows, cols = momentum.shape
         count = float(rows * cols * 8)
         sds = jax.ShapeDtypeStruct
-
-        def call(kernel, name, cost, *outs):
-            return pl.pallas_call(
-                kernel,
-                out_shape=outs if len(outs) > 1 else outs[0],
-                compiler_params=pltpu.CompilerParams(vmem_limit_bytes=24 * 1024 * 1024),
-                cost_estimate=pl.CostEstimate(flops=cost, bytes_accessed=2 * momentum.size * 4, transcendentals=0),
-                name=name,
-            )
 
         shapes = (momentum.shape, f32), (gradient.shape, bf16), ((GROUP, LANES), f32), ((2 * LANES, 2 * LANES), bf16), ((2 * LANES, 2 * LANES), bf16)
         hbm = lambda x: pltpu.with_memory_space_constraint(x, pltpu.HBM)
@@ -201,31 +197,39 @@
             compiler_params=pltpu.CompilerParams(vmem_limit_bytes=24 * 1024 * 1024),
             name="squares",
         )(hbm(momentum), hbm(gradient), hbm(kept_index.reshape(1, GROUP)))
-        squares = exchange(squares, ("core",) + mp)
-        coded = call(code_kernel, "transforms", 1 << 28, sds((8, cols), f32))(momentum, gradient, pick, code)
+        squares = exchange(squares, ("core",) + mp, first_groups)
+        vmem = lambda *shapes: tuple(pltpu.VMEM(*s) for s in shapes)
+        room = pltpu.CompilerParams(vmem_limit_bytes=24 * 1024 * 1024)
+        coded, rest_mom, rest_grad = pl.pallas_call(
+            code_kernel,
+            out_shape=vmem(((8, cols), f32), (momentum.shape, f32), (momentum.shape, f32)),
+            out_specs=(pl.BlockSpec(memory_space=pltpu.VMEM),) * 3,
+            compiler_params=room,
+            cost_estimate=pl.CostEstimate(flops=1 << 28, bytes_accessed=1 << 22, transcendentals=0),
+            name="transforms",
+        )(momentum, gradient, pick, code, decode)
         coded = lax.all_gather(coded, "core")
-        copies, own, clip = pl.pallas_call(
+        copies, clip = pl.pallas_call(
             lambda *refs: spectra_kernel(count, *refs),
-            out_shape=(pltpu.HBM((32, 2, cols), f32), pltpu.VMEM((4, cols), f32), pltpu.VMEM((8, LANES), f32)),
-            out_specs=(pl.BlockSpec(memory_space=pltpu.HBM),) + (pl.BlockSpec(memory_space=pltpu.VMEM),) * 2,
-            scratch_shapes=[pltpu.VMEM((8, 2, cols), f32), pltpu.SemaphoreType.DMA((4,))],
-            compiler_params=pltpu.CompilerParams(vmem_limit_bytes=24 * 1024 * 1024),
+            out_shape=vmem(((32, 2, cols), f32), ((8, LANES), f32)),
+            out_specs=(pl.BlockSpec(memory_space=pltpu.VMEM),) * 2,
+            compiler_params=room,
             name="spectra",
         )(squares, coded)
-        got = exchange(copies, ("z", "yh"))
-        new = call(momentum_kernel, "new_momentum", 1 << 28, sds(momentum.shape, f32))(
-            momentum, gradient, clip, own, pick, decode
-        )
+        got = exchange(copies, rep, second_groups)
         total = lax.all_gather(jnp.sum(got, axis=0), "core", tiled=True)
-        update = pl.pallas_call(
-            update_kernel,
-            out_shape=pltpu.HBM((layers, rows, cols), bf16),
-            out_specs=pl.BlockSpec(memory_space=pltpu.HBM),
-            scratch_shapes=[pltpu.VMEM((layers, rows, cols), bf16), pltpu.SemaphoreType.DMA((cols // LANES,))],
-            compiler_params=pltpu.CompilerParams(vmem_limit_bytes=24 * 1024 * 1024),
-            name="update",
-        )(total, pick, decode)
-        return new, update
+        return pl.pallas_call(
+            last_kernel,
+            out_shape=(pltpu.HBM(momentum.shape, f32), pltpu.HBM((layers, rows, cols), bf16)),
+            out_specs=(pl.BlockSpec(memory_space=pltpu.HBM),) * 2,
+            scratch_shapes=[
+                pltpu.VMEM(momentum.shape, f32),
+                pltpu.VMEM((layers, rows, cols), bf16),
+                pltpu.SemaphoreType.DMA((layers + cols // LANES,)),
+            ],
+            compiler_params=room,
+            name="new_momentum_and_update",
+        )(rest_mom, rest_grad, clip, total, pick, decode)
 
     return jax.shard_map(
         per_device,

time: 47.2 us -> 40.7 us (0.86)
  blocking collectives: 5.38 us -> 22.8 us
  waiting for transfers between devices: 13.7 us -> 0.01 us
  starting transfers between devices: 21.7 us -> 12.2 us
  Pallas kernels: 5.47 us -> 4.63 us
    all_to_all x0 -> x1, blocking collectives: none -> 18.5 us  [exchange(): return lax.all_to_all(x, axes, 0, 0, axis_index_groups=groups, tiled=True)]
    all_to_all x2 -> x1, waiting for transfers between devices: 13.7 us -> 0.01 us  [exchange(): return lax.all_to_all(x, axes, 0, 0, axis_index_groups=groups, tiled=True)]
    all_to_all x2 -> x1, starting transfers between devices: 21.7 us -> 12.2 us  [exchange(): return lax.all_to_all(x, axes, 0, 0, axis_index_groups=groups, tiled=True)]
    all_gather x1, blocking collectives: 3.55 us -> 2.48 us  [per_device(): total = lax.all_gather(jnp.sum(got, axis=0), 'core', tiled=True)]
    pallas_call x4 -> x3, Pallas kernels: 3.77 us -> 2.93 us  [the longest x1 1.44 us: per_device(): pl.pallas_call(last_kernel, out_shape=(pltpu.HBM(momentum.shape, f32), pl...]
  transfers between devices with their start and end apart: 2 -> 1, of which waited for: 2 -> 0; matrix products, arithmetic and copies ran while one was open for 0% -> 0% of each run, Pallas kernels for 4% -> 3%
where the time goes in v4:
time: 40.7 us; the launch traced here: 40.4 us
  blocking collectives  22.8 us (56%)
  starting transfers between devices  12.2 us (30%)
  Pallas kernels  4.63 us (11%)
  between operations  0.65 us (2%)
    all_to_all x1, blocking collectives, exchange(): return lax.all_to_all(x, axes, 0, 0, axis_index_groups=groups, tiled=True)  18.5 us
    all_to_all x1, starting transfers between devices, exchange(): return lax.all_to_all(x, axes, 0, 0, axis_index_groups=groups, tiled=True)  12.2 us
    all_gather x1, blocking collectives, per_device(): total = lax.all_gather(jnp.sum(got, axis=0), 'core', tiled=True)  2.48 us
    all_gather x1, blocking collectives, per_device(): coded = lax.all_gather(coded, 'core')  1.85 us
    pallas_call x1, Pallas kernels, per_device(): pl.pallas_call(first_kernel, in_specs=[pl.BlockSpec(memory_space=pltpu.HB...  1.71 us
    pallas_call x1, Pallas kernels, per_device(): pl.pallas_call(last_kernel, out_shape=(pltpu.HBM(momentum.shape, f32), pl...  1.44 us
    pallas_call x1, Pallas kernels, per_device(): pl.pallas_call(code_kernel, out_shape=vmem(((8, cols), f32), (momentum.sh...  1.3 us
  transfers between devices with their start and end apart: 1, of which 0 were waited for; matrix products, arithmetic and copies ran while one was open for 0% of the time, Pallas kernels for 3%

profile of v4, /device:TPU:1, one launch (start us, length us, event | category | flops | bytes accessed | tf_op | source)
XLA Modules:
  0.0 40.4 jit_solution(5676830975476656868)
XLA Ops:
  0.6 1.7 %squares.1 = (f32[16,8,128]{2,1,0:T(8,128)}, f32[1,2,128,640]{3,2,1,0:T(8,128)S(1)}, bf16[1,2,128,640]{3,2,1,0:T(8,128)(2,1)S(1)}, f32[64,128]{1,0:T(8,128)S(1)}...) custom-call(f32[1,2,128,640]{3,2,1,0:T(8,128)} %mom_hbm.1, bf16[1,2,128,640]{3,2,1,0:T(8,128)(2,1)} %grad_hbm.1, ...), custom_call_target="tpu_custom_call" | custom-call | tf_op jit(solution)/shard_map/squares/pallas_call | solution.py:187
  2.3 12.2 %all-to-all-start = ((f32[16,8,128]{2,1,0:T(8,128)}), f32[16,8,128]{2,1,0:T(8,128)S(1)}, u32[]{:S(2)}, u32[]{:S(2)}) async-start(f32[16,8,128]{2,1,0:T(8,128)} %get-tuple-element.20), calls=%async_computation | async-start | bytes 131072 | tf_op jit(solution)/shard_map/all_to_all | solution.py:168
  14.6 1.3 %transforms.1 = (f32[8,640]{1,0:T(8,128)S(1)}, f32[1,2,128,640]{3,2,1,0:T(8,128)S(1)}, f32[1,2,128,640]{3,2,1,0:T(8,128)S(1)}) custom-call(f32[1,2,128,640]{3,2,1,0:T(8,128)S(1)} %get-tuple-element.13.mom_ref, bf16[1,2,128,640]{3,2,1,0:T(8,128)(2,1)S(1)} %get-tuple-element.14.grad_ref, f32[64,128]{1,0:T(8,128)S(1)} %get-tuple-element.15.pick_ref, ...), custom_call_target="tpu_custom_call" | custom-call | flops 268435456 | bytes 4194304 | tf_op jit(solution)/shard_map/transforms/pallas_call | solution.py:203
  15.9 1.9 %all-gather = f32[16,640]{1,0:T(8,128)S(1)} all-gather(f32[8,640]{1,0:T(8,128)S(1)} %get-tuple-element.21), channel_id=2, replica_groups=mesh['z'=8,'yh'=4,'core'=2,'yl'=2,'x'=4] {'core'}, dimensions={0}, use_global_device_ids=true | all-gather | bytes 61440 | tf_op jit(solution)/shard_map/all_gather | solution.py:211
  17.8 0.0 all-to-all-done.refs_0_
  17.8 0.2 spectra.1
  18.0 18.5 %all_to_all.10 = f32[32,2,640]{2,1,0:T(2,128)S(1)} all-to-all(f32[32,2,640]{2,1,0:T(2,128)S(1)} %get-tuple-element.23), channel_id=1, replica_groups={{416,432,384,400,480,496,448,464,32,48,0,16,96,112,64,80,160,176,128,14..., dimensions={0} | all-to-all | bytes 327680 | tf_op jit(solution)/shard_map/all_to_all | solution.py:168
  36.4 0.1 reduce_sum.9
  36.5 2.5 %all-gather.1 = f32[2,2,640]{2,1,0:T(2,128)S(1)} all-gather(f32[1,2,640]{2,1,0:T(2,128)S(1)} %bitcast.4), channel_id=1, replica_groups=mesh['z'=8,'yh'=4,'core'=2,'yl'=2,'x'=4] {'core'}, dimensions={0}, use_global_device_ids=true | all-gather | bytes 15360 | tf_op jit(solution)/shard_map/all_gather | solution.py:220
  39.0 1.4 %new_momentum_and_update.1 = (f32[1,2,128,640]{3,2,1,0:T(8,128)}, bf16[2,128,640]{2,1,0:T(8,128)(2,1)}) custom-call(f32[1,2,128,640]{3,2,1,0:T(8,128)S(1)} %get-tuple-element.18.rest_mom_ref, f32[1,2,128,640]{3,2,1,0:T(8,128)S(1)} %get-tuple-element.19.rest_grad_ref, f32[8,128]{1,0:T(8,128)S(1)} %get-tuple-element.22.clip_ref, ...), custom_call_target="tpu_custom_call" | custom-call | tf_op jit(solution)/shard_map/new_momentum_and_update/pallas_call | solution.py:221
  (1 shorter events, 0.0 us)
Async XLA Ops:
  2.3 15.4 %all-to-all-start = ((f32[16,8,128]{2,1,0:T(8,128)}), f32[16,8,128]{2,1,0:T(8,128)S(1)}, u32[]{:S(2)}, u32[]{:S(2)}) async-start(f32[16,8,128]{2,1,0:T(8,128)} %get-tuple-element.20), calls=%async_computation | async-start | bytes 131072 | tf_op jit(solution)/shard_map/all_to_all | solution.py:168

commit v5 on v4

--- a/solution.py
+++ b/solution.py
@@ -82,8 +82,8 @@
         total = parts[:, 0:LANES]
         for b in range(1, wide.shape[1] // LANES):
             total = total + parts[:, b * LANES : (b + 1) * LANES]
-        total = total[0:4] + total[4:8]
-        squares_ref[:, 4 * layer : 4 * layer + 4] = jnp.broadcast_to(total[None], (squares_ref.shape[0], 4, LANES))
+        total = jnp.sum(total, axis=0, keepdims=True)
+        squares_ref[:, layer : layer + 1] = jnp.broadcast_to(total[None], (squares_ref.shape[0], 1, LANES))
     out = pltpu.make_async_copy(squares_ref, squares_hbm, sems.at[layers + 2])
     out.start()
     copies[-1].wait()
@@ -121,7 +121,7 @@
     members = squares_ref.shape[0] // 2
     for core in range(2):
         total = jnp.sum(squares_ref[core * members : (core + 1) * members], axis=0)
-        squares = [jnp.sum(total[i : i + 4], keepdims=True) for i in (0, 4)]
+        squares = [jnp.sum(total[i : i + 1], keepdims=True) for i in range(2)]
         square = jnp.concatenate([jnp.broadcast_to(s, (4, LANES)) for s in squares], axis=0)
         clips.append(1.0 / jnp.maximum(1.0, jnp.sqrt(square / count + epsilon)))
     clip_ref[...] = jnp.where(here == 0, clips[0], clips[1])
@@ -172,7 +172,7 @@
     whole = Mesh(mesh.devices.reshape(8, 4, 2, 2, 4), ("z", "yh", "core", "yl", "x"))
     rep, mp = ("z", "yh", "core"), ("yl", "x")
 
-    first_groups = [[core * 8 + (yl ^ 1) * 4 + (x + 2) % 4 for core in range(2) for yl in range(2) for x in range(4)]]
+    first_groups = [[core * 8 + yl * 4 + (x + 2) % 4 for core in range(2) for yl in range(2) for x in range(4)]]
     second_groups = [
         [(((z + 6) % 8) * 4 + (yh + 2) % 4) * 2 + core for z in range(8) for yh in range(4)] for core in range(2)
     ]
@@ -187,10 +187,10 @@
         squares, momentum, gradient, pick, code, decode = pl.pallas_call(
             first_kernel,
             in_specs=[pl.BlockSpec(memory_space=pltpu.HBM)] * 3,
-            out_shape=(pltpu.HBM((16, 8, LANES), f32), *[pltpu.VMEM(*s) for s in shapes]),
+            out_shape=(pltpu.HBM((16, 2, LANES), f32), *[pltpu.VMEM(*s) for s in shapes]),
             out_specs=(pl.BlockSpec(memory_space=pltpu.HBM),) + (pl.BlockSpec(memory_space=pltpu.VMEM),) * 5,
             scratch_shapes=[
-                pltpu.VMEM((16, 8, LANES), f32),
+                pltpu.VMEM((16, 2, LANES), f32),
                 pltpu.VMEM((1, GROUP), jnp.int32),
                 pltpu.SemaphoreType.DMA((layers + 3,)),
             ],

time: 40.7 us -> 40.6 us (level)
  starting transfers between devices: 12.2 us -> 11.3 us
  blocking collectives: 22.8 us -> 23.6 us
    all_to_all x1, starting transfers between devices: 12.2 us -> 11.3 us  [exchange(): return lax.all_to_all(x, axes, 0, 0, axis_index_groups=groups, tiled=True)]
    all_to_all x1, blocking collectives: 18.5 us -> 19.3 us  [exchange(): return lax.all_to_all(x, axes, 0, 0, axis_index_groups=groups, tiled=True)]
  transfers between devices with their start and end apart: 1 -> 1, of which waited for: 0 -> 1; matrix products, arithmetic and copies ran while one was open for 0% -> 0% of each run, Pallas kernels for 3% -> 3%
where the time goes in v5:
time: 40.6 us; the launch traced here: 40.3 us
  blocking collectives  23.6 us (58%)
  starting transfers between devices  11.3 us (28%)
  Pallas kernels  4.61 us (11%)
  between operations  0.65 us (2%)
    all_to_all x1, blocking collectives, exchange(): return lax.all_to_all(x, axes, 0, 0, axis_index_groups=groups, tiled=True)  19.3 us
    all_to_all x1, starting transfers between devices, exchange(): return lax.all_to_all(x, axes, 0, 0, axis_index_groups=groups, tiled=True)  11.3 us
    all_gather x1, blocking collectives, per_device(): total = lax.all_gather(jnp.sum(got, axis=0), 'core', tiled=True)  2.45 us
    all_gather x1, blocking collectives, per_device(): coded = lax.all_gather(coded, 'core')  1.86 us
    pallas_call x1, Pallas kernels, per_device(): pl.pallas_call(first_kernel, in_specs=[pl.BlockSpec(memory_space=pltpu.HB...  1.69 us
    pallas_call x1, Pallas kernels, per_device(): pl.pallas_call(last_kernel, out_shape=(pltpu.HBM(momentum.shape, f32), pl...  1.44 us
    pallas_call x1, Pallas kernels, per_device(): pl.pallas_call(code_kernel, out_shape=vmem(((8, cols), f32), (momentum.sh...  1.29 us
  transfers between devices with their start and end apart: 1, of which 1 were waited for; matrix products, arithmetic and copies ran while one was open for 0% of the time, Pallas kernels for 3%

profile of v5, /device:TPU:1, one launch (start us, length us, event | category | flops | bytes accessed | tf_op | source)
XLA Modules:
  0.0 40.3 jit_solution(16293349749284515540)
XLA Ops:
  0.6 1.7 %squares.1 = (f32[16,2,128]{2,1,0:T(2,128)}, f32[1,2,128,640]{3,2,1,0:T(8,128)S(1)}, bf16[1,2,128,640]{3,2,1,0:T(8,128)(2,1)S(1)}, f32[64,128]{1,0:T(8,128)S(1)}...) custom-call(f32[1,2,128,640]{3,2,1,0:T(8,128)} %mom_hbm.1, bf16[1,2,128,640]{3,2,1,0:T(8,128)(2,1)} %grad_hbm.1, ...), custom_call_target="tpu_custom_call" | custom-call | tf_op jit(solution)/shard_map/squares/pallas_call | solution.py:187
  2.3 11.3 %all-to-all-start = ((f32[16,2,128]{2,1,0:T(2,128)}), f32[16,2,128]{2,1,0:T(2,128)S(1)}, u32[]{:S(2)}, u32[]{:S(2)}) async-start(f32[16,2,128]{2,1,0:T(2,128)} %get-tuple-element.20), calls=%async_computation | async-start | bytes 32768 | tf_op jit(solution)/shard_map/all_to_all | solution.py:168
  13.7 1.3 %transforms.1 = (f32[8,640]{1,0:T(8,128)S(1)}, f32[1,2,128,640]{3,2,1,0:T(8,128)S(1)}, f32[1,2,128,640]{3,2,1,0:T(8,128)S(1)}) custom-call(f32[1,2,128,640]{3,2,1,0:T(8,128)S(1)} %get-tuple-element.13.mom_ref, bf16[1,2,128,640]{3,2,1,0:T(8,128)(2,1)S(1)} %get-tuple-element.14.grad_ref, f32[64,128]{1,0:T(8,128)S(1)} %get-tuple-element.15.pick_ref, ...), custom_call_target="tpu_custom_call" | custom-call | flops 268435456 | bytes 4194304 | tf_op jit(solution)/shard_map/transforms/pallas_call | solution.py:203
  15.0 1.9 %all-gather = f32[16,640]{1,0:T(8,128)S(1)} all-gather(f32[8,640]{1,0:T(8,128)S(1)} %get-tuple-element.21), channel_id=2, replica_groups=mesh['z'=8,'yh'=4,'core'=2,'yl'=2,'x'=4] {'core'}, dimensions={0}, use_global_device_ids=true | all-gather | bytes 61440 | tf_op jit(solution)/shard_map/all_gather | solution.py:211
  16.8 0.1 all-to-all-done.refs_0_
  16.9 0.2 spectra.1
  17.1 19.3 %all_to_all.10 = f32[32,2,640]{2,1,0:T(2,128)S(1)} all-to-all(f32[32,2,640]{2,1,0:T(2,128)S(1)} %get-tuple-element.23), channel_id=1, replica_groups={{416,432,384,400,480,496,448,464,32,48,0,16,96,112,64,80,160,176,128,14..., dimensions={0} | all-to-all | bytes 327680 | tf_op jit(solution)/shard_map/all_to_all | solution.py:168
  36.4 0.1 reduce_sum.9
  36.4 2.4 %all-gather.1 = f32[2,2,640]{2,1,0:T(2,128)S(1)} all-gather(f32[1,2,640]{2,1,0:T(2,128)S(1)} %bitcast.4), channel_id=1, replica_groups=mesh['z'=8,'yh'=4,'core'=2,'yl'=2,'x'=4] {'core'}, dimensions={0}, use_global_device_ids=true | all-gather | bytes 15360 | tf_op jit(solution)/shard_map/all_gather | solution.py:220
  38.9 1.4 %new_momentum_and_update.1 = (f32[1,2,128,640]{3,2,1,0:T(8,128)}, bf16[2,128,640]{2,1,0:T(8,128)(2,1)}) custom-call(f32[1,2,128,640]{3,2,1,0:T(8,128)S(1)} %get-tuple-element.18.rest_mom_ref, f32[1,2,128,640]{3,2,1,0:T(8,128)S(1)} %get-tuple-element.19.rest_grad_ref, f32[8,128]{1,0:T(8,128)S(1)} %get-tuple-element.22.clip_ref, ...), custom_call_target="tpu_custom_call" | custom-call | tf_op jit(solution)/shard_map/new_momentum_and_update/pallas_call | solution.py:221
  (1 shorter events, 0.0 us)
Async XLA Ops:
  2.3 14.6 %all-to-all-start = ((f32[16,2,128]{2,1,0:T(2,128)}), f32[16,2,128]{2,1,0:T(2,128)S(1)}, u32[]{:S(2)}, u32[]{:S(2)}) async-start(f32[16,2,128]{2,1,0:T(2,128)} %get-tuple-element.20), calls=%async_computation | async-start | bytes 32768 | tf_op jit(solution)/shard_map/all_to_all | solution.py:168

commit v6 on v5

--- a/solution.py
+++ b/solution.py
@@ -63,6 +63,18 @@
     for copy in copies:
         copy.start()
 
+    for layer in range(layers):
+        copies[layer].wait()
+        wide = grad_ref[0, layer].astype(f32)
+        parts = jnp.sum((wide * wide).reshape(-1, 8, wide.shape[1]), axis=0)
+        total = parts[:, 0:LANES]
+        for b in range(1, wide.shape[1] // LANES):
+            total = total + parts[:, b * LANES : (b + 1) * LANES]
+        total = jnp.sum(total, axis=0, keepdims=True)
+        squares_ref[:, layer : layer + 1] = jnp.broadcast_to(total[None], (squares_ref.shape[0], 1, LANES))
+    out = pltpu.make_async_copy(squares_ref, squares_hbm, sems.at[layers + 2])
+    out.start()
+
     copies[layers].wait()
     kept = kept_ref[...]
     kept = jnp.concatenate([kept, kept], axis=1)
@@ -74,18 +86,6 @@
     high, low = halves(both)
     code_ref[...] = joined(high, low)
     decode_ref[...] = joined(high, low, transposed=True)
-
-    for layer in range(layers):
-        copies[layer].wait()
-        wide = grad_ref[0, layer].astype(f32)
-        parts = jnp.sum((wide * wide).reshape(-1, 8, wide.shape[1]), axis=0)
-        total = parts[:, 0:LANES]
-        for b in range(1, wide.shape[1] // LANES):
-            total = total + parts[:, b * LANES : (b + 1) * LANES]
-        total = jnp.sum(total, axis=0, keepdims=True)
-        squares_ref[:, layer : layer + 1] = jnp.broadcast_to(total[None], (squares_ref.shape[0], 1, LANES))
-    out = pltpu.make_async_copy(squares_ref, squares_hbm, sems.at[layers + 2])
-    out.start()
     copies[-1].wait()
     out.wait()
 

time: 40.6 us -> 40.6 us (level)
  no operation moved by 1% of the time
where the time goes in v6:
time: 40.6 us; the launch traced here: 40.3 us
  blocking collectives  23.6 us (58%)
  starting transfers between devices  11.3 us (28%)
  Pallas kernels  4.61 us (11%)
  between operations  0.65 us (2%)
    all_to_all x1, blocking collectives, exchange(): return lax.all_to_all(x, axes, 0, 0, axis_index_groups=groups, tiled=True)  19.3 us
    all_to_all x1, starting transfers between devices, exchange(): return lax.all_to_all(x, axes, 0, 0, axis_index_groups=groups, tiled=True)  11.3 us
    all_gather x1, blocking collectives, per_device(): total = lax.all_gather(jnp.sum(got, axis=0), 'core', tiled=True)  2.45 us
    all_gather x1, blocking collectives, per_device(): coded = lax.all_gather(coded, 'core')  1.86 us
    pallas_call x1, Pallas kernels, per_device(): pl.pallas_call(first_kernel, in_specs=[pl.BlockSpec(memory_space=pltpu.HB...  1.68 us
    pallas_call x1, Pallas kernels, per_device(): pl.pallas_call(last_kernel, out_shape=(pltpu.HBM(momentum.shape, f32), pl...  1.44 us
    pallas_call x1, Pallas kernels, per_device(): pl.pallas_call(code_kernel, out_shape=vmem(((8, cols), f32), (momentum.sh...  1.3 us
  transfers between devices with their start and end apart: 1, of which 1 were waited for; matrix products, arithmetic and copies ran while one was open for 0% of the time, Pallas kernels for 3%

profile of v6, /device:TPU:1, one launch (start us, length us, event | category | flops | bytes accessed | tf_op | source)
XLA Modules:
  0.0 40.3 jit_solution(14155940778125630064)
XLA Ops:
  0.6 1.7 %squares.1 = (f32[16,2,128]{2,1,0:T(2,128)}, f32[1,2,128,640]{3,2,1,0:T(8,128)S(1)}, bf16[1,2,128,640]{3,2,1,0:T(8,128)(2,1)S(1)}, f32[64,128]{1,0:T(8,128)S(1)}...) custom-call(f32[1,2,128,640]{3,2,1,0:T(8,128)} %mom_hbm.1, bf16[1,2,128,640]{3,2,1,0:T(8,128)(2,1)} %grad_hbm.1, ...), custom_call_target="tpu_custom_call" | custom-call | tf_op jit(solution)/shard_map/squares/pallas_call | solution.py:187
  2.3 11.3 %all-to-all-start = ((f32[16,2,128]{2,1,0:T(2,128)}), f32[16,2,128]{2,1,0:T(2,128)S(1)}, u32[]{:S(2)}, u32[]{:S(2)}) async-start(f32[16,2,128]{2,1,0:T(2,128)} %get-tuple-element.20), calls=%async_computation | async-start | bytes 32768 | tf_op jit(solution)/shard_map/all_to_all | solution.py:168
  13.7 1.3 %transforms.1 = (f32[8,640]{1,0:T(8,128)S(1)}, f32[1,2,128,640]{3,2,1,0:T(8,128)S(1)}, f32[1,2,128,640]{3,2,1,0:T(8,128)S(1)}) custom-call(f32[1,2,128,640]{3,2,1,0:T(8,128)S(1)} %get-tuple-element.13.mom_ref, bf16[1,2,128,640]{3,2,1,0:T(8,128)(2,1)S(1)} %get-tuple-element.14.grad_ref, f32[64,128]{1,0:T(8,128)S(1)} %get-tuple-element.15.pick_ref, ...), custom_call_target="tpu_custom_call" | custom-call | flops 268435456 | bytes 4194304 | tf_op jit(solution)/shard_map/transforms/pallas_call | solution.py:203
  15.0 1.9 %all-gather = f32[16,640]{1,0:T(8,128)S(1)} all-gather(f32[8,640]{1,0:T(8,128)S(1)} %get-tuple-element.21), channel_id=2, replica_groups=mesh['z'=8,'yh'=4,'core'=2,'yl'=2,'x'=4] {'core'}, dimensions={0}, use_global_device_ids=true | all-gather | bytes 61440 | tf_op jit(solution)/shard_map/all_gather | solution.py:211
  16.8 0.1 all-to-all-done.refs_0_
  16.9 0.2 spectra.1
  17.1 19.3 %all_to_all.10 = f32[32,2,640]{2,1,0:T(2,128)S(1)} all-to-all(f32[32,2,640]{2,1,0:T(2,128)S(1)} %get-tuple-element.23), channel_id=1, replica_groups={{416,432,384,400,480,496,448,464,32,48,0,16,96,112,64,80,160,176,128,14..., dimensions={0} | all-to-all | bytes 327680 | tf_op jit(solution)/shard_map/all_to_all | solution.py:168
  36.4 0.1 reduce_sum.9
  36.4 2.4 %all-gather.1 = f32[2,2,640]{2,1,0:T(2,128)S(1)} all-gather(f32[1,2,640]{2,1,0:T(2,128)S(1)} %bitcast.4), channel_id=1, replica_groups=mesh['z'=8,'yh'=4,'core'=2,'yl'=2,'x'=4] {'core'}, dimensions={0}, use_global_device_ids=true | all-gather | bytes 15360 | tf_op jit(solution)/shard_map/all_gather | solution.py:220
  38.9 1.4 %new_momentum_and_update.1 = (f32[1,2,128,640]{3,2,1,0:T(8,128)}, bf16[2,128,640]{2,1,0:T(8,128)(2,1)}) custom-call(f32[1,2,128,640]{3,2,1,0:T(8,128)S(1)} %get-tuple-element.18.rest_mom_ref, f32[1,2,128,640]{3,2,1,0:T(8,128)S(1)} %get-tuple-element.19.rest_grad_ref, f32[8,128]{1,0:T(8,128)S(1)} %get-tuple-element.22.clip_ref, ...), custom_call_target="tpu_custom_call" | custom-call | tf_op jit(solution)/shard_map/new_momentum_and_update/pallas_call | solution.py:221
  (1 shorter events, 0.0 us)
Async XLA Ops:
  2.3 14.6 %all-to-all-start = ((f32[16,2,128]{2,1,0:T(2,128)}), f32[16,2,128]{2,1,0:T(2,128)S(1)}, u32[]{:S(2)}, u32[]{:S(2)}) async-start(f32[16,2,128]{2,1,0:T(2,128)} %get-tuple-element.20), calls=%async_computation | async-start | bytes 32768 | tf_op jit(solution)/shard_map/all_to_all | solution.py:168

commit v7 on v6

--- a/solution.py
+++ b/solution.py
@@ -9,6 +9,7 @@
 
 GROUP = 64
 LANES = 128
+CHUNK = 32
 decay_rate = 0.999
 epsilon = 1e-06
 f32 = jnp.float32
@@ -141,12 +142,14 @@
     layers, rows, cols = update_ref.shape
     copies = []
     for layer in range(layers):
-        for b in range(cols // LANES):
-            lanes = slice(b * LANES, (b + 1) * LANES)
-            each = clip_ref[4 * layer : 4 * layer + 1, :]
-            new_ref[0, layer, :, lanes] = rest_mom_ref[0, layer, :, lanes] + (each * rest_grad_ref[0, layer, :, lanes]) * SHIFT
-        copies.append(pltpu.make_async_copy(new_ref.at[:, layer], new_hbm.at[:, layer], sems.at[layer]))
-        copies[-1].start()
+        each = clip_ref[4 * layer : 4 * layer + 1, :]
+        for start in range(0, rows, CHUNK):
+            part = pl.ds(start, CHUNK)
+            for b in range(cols // LANES):
+                lanes = pl.ds(b * LANES, LANES)
+                new_ref[0, layer, part, lanes] = rest_mom_ref[0, layer, part, lanes] + (each * rest_grad_ref[0, layer, part, lanes]) * SHIFT
+            copies.append(pltpu.make_async_copy(new_ref.at[:, layer, part], new_hbm.at[:, layer, part], sems.at[len(copies)]))
+            copies[-1].start()
     lane = lax.broadcasted_iota(jnp.int32, (4, LANES), 1)
     for b in range(cols // LANES):
         lanes = slice(b * LANES, (b + 1) * LANES)
@@ -158,7 +161,7 @@
         scale = 1.0 / (mean + epsilon)
         update_ref[:, :, lanes] = jnp.tanh(tiles * scale[:, None, :]).astype(bf16).reshape(layers, rows, LANES)
         part = pl.ds(b * LANES, LANES)
-        copies.append(pltpu.make_async_copy(update_ref.at[:, :, part], update_hbm.at[:, :, part], sems.at[layers + b]))
+        copies.append(pltpu.make_async_copy(update_ref.at[:, :, part], update_hbm.at[:, :, part], sems.at[len(copies)]))
         copies[-1].start()
     for copy in copies:
         copy.wait()
@@ -225,7 +228,7 @@
             scratch_shapes=[
                 pltpu.VMEM(momentum.shape, f32),
                 pltpu.VMEM((layers, rows, cols), bf16),
-                pltpu.SemaphoreType.DMA((layers + cols // LANES,)),
+                pltpu.SemaphoreType.DMA((layers * (rows // CHUNK) + cols // LANES,)),
             ],
             compiler_params=room,
             name="new_momentum_and_update",

time: 40.6 us -> 40.6 us (level)
  no operation moved by 1% of the time
where the time goes in v7:
time: 40.6 us; the launch traced here: 40.3 us
  blocking collectives  23.6 us (58%)
  starting transfers between devices  11.3 us (28%)
  Pallas kernels  4.6 us (11%)
  between operations  0.65 us (2%)
    all_to_all x1, blocking collectives, exchange(): return lax.all_to_all(x, axes, 0, 0, axis_index_groups=groups, tiled=True)  19.3 us
    all_to_all x1, starting transfers between devices, exchange(): return lax.all_to_all(x, axes, 0, 0, axis_index_groups=groups, tiled=True)  11.3 us
    all_gather x1, blocking collectives, per_device(): total = lax.all_gather(jnp.sum(got, axis=0), 'core', tiled=True)  2.45 us
    all_gather x1, blocking collectives, per_device(): coded = lax.all_gather(coded, 'core')  1.86 us
    pallas_call x1, Pallas kernels, per_device(): pl.pallas_call(first_kernel, in_specs=[pl.BlockSpec(memory_space=pltpu.HB...  1.68 us
    pallas_call x1, Pallas kernels, per_device(): pl.pallas_call(last_kernel, out_shape=(pltpu.HBM(momentum.shape, f32), pl...  1.43 us
    pallas_call x1, Pallas kernels, per_device(): pl.pallas_call(code_kernel, out_shape=vmem(((8, cols), f32), (momentum.sh...  1.3 us
  transfers between devices with their start and end apart: 1, of which 1 were waited for; matrix products, arithmetic and copies ran while one was open for 0% of the time, Pallas kernels for 3%

profile of v7, /device:TPU:1, one launch (start us, length us, event | category | flops | bytes accessed | tf_op | source)
XLA Modules:
  0.0 40.3 jit_solution(5220757649576247479)
XLA Ops:
  0.6 1.7 %squares.1 = (f32[16,2,128]{2,1,0:T(2,128)}, f32[1,2,128,640]{3,2,1,0:T(8,128)S(1)}, bf16[1,2,128,640]{3,2,1,0:T(8,128)(2,1)S(1)}, f32[64,128]{1,0:T(8,128)S(1)}...) custom-call(f32[1,2,128,640]{3,2,1,0:T(8,128)} %mom_hbm.1, bf16[1,2,128,640]{3,2,1,0:T(8,128)(2,1)} %grad_hbm.1, ...), custom_call_target="tpu_custom_call" | custom-call | tf_op jit(solution)/shard_map/squares/pallas_call | solution.py:190
  2.3 11.3 %all-to-all-start = ((f32[16,2,128]{2,1,0:T(2,128)}), f32[16,2,128]{2,1,0:T(2,128)S(1)}, u32[]{:S(2)}, u32[]{:S(2)}) async-start(f32[16,2,128]{2,1,0:T(2,128)} %get-tuple-element.20), calls=%async_computation | async-start | bytes 32768 | tf_op jit(solution)/shard_map/all_to_all | solution.py:171
  13.7 1.3 %transforms.1 = (f32[8,640]{1,0:T(8,128)S(1)}, f32[1,2,128,640]{3,2,1,0:T(8,128)S(1)}, f32[1,2,128,640]{3,2,1,0:T(8,128)S(1)}) custom-call(f32[1,2,128,640]{3,2,1,0:T(8,128)S(1)} %get-tuple-element.13.mom_ref, bf16[1,2,128,640]{3,2,1,0:T(8,128)(2,1)S(1)} %get-tuple-element.14.grad_ref, f32[64,128]{1,0:T(8,128)S(1)} %get-tuple-element.15.pick_ref, ...), custom_call_target="tpu_custom_call" | custom-call | flops 268435456 | bytes 4194304 | tf_op jit(solution)/shard_map/transforms/pallas_call | solution.py:206
  15.0 1.9 %all-gather = f32[16,640]{1,0:T(8,128)S(1)} all-gather(f32[8,640]{1,0:T(8,128)S(1)} %get-tuple-element.21), channel_id=2, replica_groups=mesh['z'=8,'yh'=4,'core'=2,'yl'=2,'x'=4] {'core'}, dimensions={0}, use_global_device_ids=true | all-gather | bytes 61440 | tf_op jit(solution)/shard_map/all_gather | solution.py:214
  16.8 0.1 all-to-all-done.refs_0_
  16.9 0.2 spectra.1
  17.1 19.3 %all_to_all.10 = f32[32,2,640]{2,1,0:T(2,128)S(1)} all-to-all(f32[32,2,640]{2,1,0:T(2,128)S(1)} %get-tuple-element.23), channel_id=1, replica_groups={{416,432,384,400,480,496,448,464,32,48,0,16,96,112,64,80,160,176,128,14..., dimensions={0} | all-to-all | bytes 327680 | tf_op jit(solution)/shard_map/all_to_all | solution.py:171
  36.4 0.1 reduce_sum.9
  36.4 2.4 %all-gather.1 = f32[2,2,640]{2,1,0:T(2,128)S(1)} all-gather(f32[1,2,640]{2,1,0:T(2,128)S(1)} %bitcast.4), channel_id=1, replica_groups=mesh['z'=8,'yh'=4,'core'=2,'yl'=2,'x'=4] {'core'}, dimensions={0}, use_global_device_ids=true | all-gather | bytes 15360 | tf_op jit(solution)/shard_map/all_gather | solution.py:223
  38.9 1.4 %new_momentum_and_update.1 = (f32[1,2,128,640]{3,2,1,0:T(8,128)}, bf16[2,128,640]{2,1,0:T(8,128)(2,1)}) custom-call(f32[1,2,128,640]{3,2,1,0:T(8,128)S(1)} %get-tuple-element.18.rest_mom_ref, f32[1,2,128,640]{3,2,1,0:T(8,128)S(1)} %get-tuple-element.19.rest_grad_ref, f32[8,128]{1,0:T(8,128)S(1)} %get-tuple-element.22.clip_ref, ...), custom_call_target="tpu_custom_call" | custom-call | tf_op jit(solution)/shard_map/new_momentum_and_update/pallas_call | solution.py:224
  (1 shorter events, 0.0 us)
Async XLA Ops:
  2.3 14.6 %all-to-all-start = ((f32[16,2,128]{2,1,0:T(2,128)}), f32[16,2,128]{2,1,0:T(2,128)S(1)}, u32[]{:S(2)}, u32[]{:S(2)}) async-start(f32[16,2,128]{2,1,0:T(2,128)} %get-tuple-element.20), calls=%async_computation | async-start | bytes 32768 | tf_op jit(solution)/shard_map/all_to_all | solution.py:171

commit v8 on v7

--- a/solution.py
+++ b/solution.py
@@ -58,25 +58,31 @@
 
 def first_kernel(mom_hbm, grad_hbm, kept_hbm, squares_hbm, mom_ref, grad_ref, pick_ref, code_ref, decode_ref, squares_ref, kept_ref, sems):
     layers = grad_ref.shape[1]
-    copies = [pltpu.make_async_copy(grad_hbm.at[:, i], grad_ref.at[:, i], sems.at[i]) for i in range(layers)]
-    copies += [pltpu.make_async_copy(kept_hbm, kept_ref, sems.at[layers])]
-    copies += [pltpu.make_async_copy(mom_hbm, mom_ref, sems.at[layers + 1])]
+    half = grad_ref.shape[2] // 2
+    copies = []
+    for i in range(2 * layers):
+        part = (slice(None), i // 2, pl.ds(i % 2 * half, half))
+        copies.append(pltpu.make_async_copy(grad_hbm.at[part], grad_ref.at[part], sems.at[i]))
+    copies += [pltpu.make_async_copy(kept_hbm, kept_ref, sems.at[2 * layers])]
+    copies += [pltpu.make_async_copy(mom_hbm, mom_ref, sems.at[2 * layers + 1])]
     for copy in copies:
         copy.start()
 
     for layer in range(layers):
-        copies[layer].wait()
-        wide = grad_ref[0, layer].astype(f32)
-        parts = jnp.sum((wide * wide).reshape(-1, 8, wide.shape[1]), axis=0)
+        parts = 0.0
+        for i in range(2):
+            copies[2 * layer + i].wait()
+            wide = grad_ref[0, layer, i * half : (i + 1) * half].astype(f32)
+            parts = parts + jnp.sum((wide * wide).reshape(-1, 8, wide.shape[1]), axis=0)
         total = parts[:, 0:LANES]
         for b in range(1, wide.shape[1] // LANES):
             total = total + parts[:, b * LANES : (b + 1) * LANES]
         total = jnp.sum(total, axis=0, keepdims=True)
         squares_ref[:, layer : layer + 1] = jnp.broadcast_to(total[None], (squares_ref.shape[0], 1, LANES))
-    out = pltpu.make_async_copy(squares_ref, squares_hbm, sems.at[layers + 2])
+    out = pltpu.make_async_copy(squares_ref, squares_hbm, sems.at[2 * layers + 2])
     out.start()
 
-    copies[layers].wait()
+    copies[2 * layers].wait()
     kept = kept_ref[...]
     kept = jnp.concatenate([kept, kept], axis=1)
     place = lax.broadcasted_iota(jnp.int32, (GROUP, LANES), 0)
@@ -195,7 +201,7 @@
             scratch_shapes=[
                 pltpu.VMEM((16, 2, LANES), f32),
                 pltpu.VMEM((1, GROUP), jnp.int32),
-                pltpu.SemaphoreType.DMA((layers + 3,)),
+                pltpu.SemaphoreType.DMA((2 * layers + 3,)),
             ],
             compiler_params=pltpu.CompilerParams(vmem_limit_bytes=24 * 1024 * 1024),
             name="squares",

time: 40.6 us -> 40.6 us (level)
  no operation moved by 1% of the time
where the time goes in v8:
time: 40.6 us; the launch traced here: 40.3 us
  blocking collectives  23.6 us (58%)
  starting transfers between devices  11.3 us (28%)
  Pallas kernels  4.61 us (11%)
  between operations  0.65 us (2%)
    all_to_all x1, blocking collectives, exchange(): return lax.all_to_all(x, axes, 0, 0, axis_index_groups=groups, tiled=True)  19.3 us
    all_to_all x1, starting transfers between devices, exchange(): return lax.all_to_all(x, axes, 0, 0, axis_index_groups=groups, tiled=True)  11.3 us
    all_gather x1, blocking collectives, per_device(): total = lax.all_gather(jnp.sum(got, axis=0), 'core', tiled=True)  2.45 us
    all_gather x1, blocking collectives, per_device(): coded = lax.all_gather(coded, 'core')  1.85 us
    pallas_call x1, Pallas kernels, per_device(): pl.pallas_call(first_kernel, in_specs=[pl.BlockSpec(memory_space=pltpu.HB...  1.7 us
    pallas_call x1, Pallas kernels, per_device(): pl.pallas_call(last_kernel, out_shape=(pltpu.HBM(momentum.shape, f32), pl...  1.42 us
    pallas_call x1, Pallas kernels, per_device(): pl.pallas_call(code_kernel, out_shape=vmem(((8, cols), f32), (momentum.sh...  1.3 us
  transfers between devices with their start and end apart: 1, of which 1 were waited for; matrix products, arithmetic and copies ran while one was open for 0% of the time, Pallas kernels for 3%

profile of v8, /device:TPU:1, one launch (start us, length us, event | category | flops | bytes accessed | tf_op | source)
XLA Modules:
  0.0 40.3 jit_solution(6975683218959326503)
XLA Ops:
  0.6 1.7 %squares.1 = (f32[16,2,128]{2,1,0:T(2,128)}, f32[1,2,128,640]{3,2,1,0:T(8,128)S(1)}, bf16[1,2,128,640]{3,2,1,0:T(8,128)(2,1)S(1)}, f32[64,128]{1,0:T(8,128)S(1)}...) custom-call(f32[1,2,128,640]{3,2,1,0:T(8,128)} %mom_hbm.1, bf16[1,2,128,640]{3,2,1,0:T(8,128)(2,1)} %grad_hbm.1, ...), custom_call_target="tpu_custom_call" | custom-call | tf_op jit(solution)/shard_map/squares/pallas_call | solution.py:196
  2.3 11.3 %all-to-all-start = ((f32[16,2,128]{2,1,0:T(2,128)}), f32[16,2,128]{2,1,0:T(2,128)S(1)}, u32[]{:S(2)}, u32[]{:S(2)}) async-start(f32[16,2,128]{2,1,0:T(2,128)} %get-tuple-element.20), calls=%async_computation | async-start | bytes 32768 | tf_op jit(solution)/shard_map/all_to_all | solution.py:177
  13.7 1.3 %transforms.1 = (f32[8,640]{1,0:T(8,128)S(1)}, f32[1,2,128,640]{3,2,1,0:T(8,128)S(1)}, f32[1,2,128,640]{3,2,1,0:T(8,128)S(1)}) custom-call(f32[1,2,128,640]{3,2,1,0:T(8,128)S(1)} %get-tuple-element.13.mom_ref, bf16[1,2,128,640]{3,2,1,0:T(8,128)(2,1)S(1)} %get-tuple-element.14.grad_ref, f32[64,128]{1,0:T(8,128)S(1)} %get-tuple-element.15.pick_ref, ...), custom_call_target="tpu_custom_call" | custom-call | flops 268435456 | bytes 4194304 | tf_op jit(solution)/shard_map/transforms/pallas_call | solution.py:212
  15.0 1.9 %all-gather = f32[16,640]{1,0:T(8,128)S(1)} all-gather(f32[8,640]{1,0:T(8,128)S(1)} %get-tuple-element.21), channel_id=2, replica_groups=mesh['z'=8,'yh'=4,'core'=2,'yl'=2,'x'=4] {'core'}, dimensions={0}, use_global_device_ids=true | all-gather | bytes 61440 | tf_op jit(solution)/shard_map/all_gather | solution.py:220
  16.8 0.1 all-to-all-done.refs_0_
  16.9 0.2 spectra.1
  17.1 19.3 %all_to_all.10 = f32[32,2,640]{2,1,0:T(2,128)S(1)} all-to-all(f32[32,2,640]{2,1,0:T(2,128)S(1)} %get-tuple-element.23), channel_id=1, replica_groups={{416,432,384,400,480,496,448,464,32,48,0,16,96,112,64,80,160,176,128,14..., dimensions={0} | all-to-all | bytes 327680 | tf_op jit(solution)/shard_map/all_to_all | solution.py:177
  36.4 0.1 reduce_sum.9
  36.4 2.5 %all-gather.1 = f32[2,2,640]{2,1,0:T(2,128)S(1)} all-gather(f32[1,2,640]{2,1,0:T(2,128)S(1)} %bitcast.4), channel_id=1, replica_groups=mesh['z'=8,'yh'=4,'core'=2,'yl'=2,'x'=4] {'core'}, dimensions={0}, use_global_device_ids=true | all-gather | bytes 15360 | tf_op jit(solution)/shard_map/all_gather | solution.py:229
  38.9 1.4 %new_momentum_and_update.1 = (f32[1,2,128,640]{3,2,1,0:T(8,128)}, bf16[2,128,640]{2,1,0:T(8,128)(2,1)}) custom-call(f32[1,2,128,640]{3,2,1,0:T(8,128)S(1)} %get-tuple-element.18.rest_mom_ref, f32[1,2,128,640]{3,2,1,0:T(8,128)S(1)} %get-tuple-element.19.rest_grad_ref, f32[8,128]{1,0:T(8,128)S(1)} %get-tuple-element.22.clip_ref, ...), custom_call_target="tpu_custom_call" | custom-call | tf_op jit(solution)/shard_map/new_momentum_and_update/pallas_call | solution.py:230
  (1 shorter events, 0.0 us)
Async XLA Ops:
  2.3 14.6 %all-to-all-start = ((f32[16,2,128]{2,1,0:T(2,128)}), f32[16,2,128]{2,1,0:T(2,128)S(1)}, u32[]{:S(2)}, u32[]{:S(2)}) async-start(f32[16,2,128]{2,1,0:T(2,128)} %get-tuple-element.20), calls=%async_computation | async-start | bytes 32768 | tf_op jit(solution)/shard_map/all_to_all | solution.py:177

commit v9 on v6

--- a/solution.py
+++ b/solution.py
@@ -140,13 +140,6 @@
 def last_kernel(rest_mom_ref, rest_grad_ref, clip_ref, total_ref, pick_ref, decode_ref, new_hbm, update_hbm, new_ref, update_ref, sems):
     layers, rows, cols = update_ref.shape
     copies = []
-    for layer in range(layers):
-        for b in range(cols // LANES):
-            lanes = slice(b * LANES, (b + 1) * LANES)
-            each = clip_ref[4 * layer : 4 * layer + 1, :]
-            new_ref[0, layer, :, lanes] = rest_mom_ref[0, layer, :, lanes] + (each * rest_grad_ref[0, layer, :, lanes]) * SHIFT
-        copies.append(pltpu.make_async_copy(new_ref.at[:, layer], new_hbm.at[:, layer], sems.at[layer]))
-        copies[-1].start()
     lane = lax.broadcasted_iota(jnp.int32, (4, LANES), 1)
     for b in range(cols // LANES):
         lanes = slice(b * LANES, (b + 1) * LANES)
@@ -157,8 +150,13 @@
         mean = jnp.where(lane < GROUP, left, right) / (GROUP * GROUP)
         scale = 1.0 / (mean + epsilon)
         update_ref[:, :, lanes] = jnp.tanh(tiles * scale[:, None, :]).astype(bf16).reshape(layers, rows, LANES)
+        for layer in range(layers):
+            each = clip_ref[4 * layer : 4 * layer + 1, :]
+            new_ref[0, layer, :, lanes] = rest_mom_ref[0, layer, :, lanes] + (each * rest_grad_ref[0, layer, :, lanes]) * SHIFT
         part = pl.ds(b * LANES, LANES)
-        copies.append(pltpu.make_async_copy(update_ref.at[:, :, part], update_hbm.at[:, :, part], sems.at[layers + b]))
+        copies.append(pltpu.make_async_copy(new_ref.at[:, :, :, part], new_hbm.at[:, :, :, part], sems.at[len(copies)]))
+        copies[-1].start()
+        copies.append(pltpu.make_async_copy(update_ref.at[:, :, part], update_hbm.at[:, :, part], sems.at[len(copies)]))
         copies[-1].start()
     for copy in copies:
         copy.wait()
@@ -225,7 +223,7 @@
             scratch_shapes=[
                 pltpu.VMEM(momentum.shape, f32),
                 pltpu.VMEM((layers, rows, cols), bf16),
-                pltpu.SemaphoreType.DMA((layers + cols // LANES,)),
+                pltpu.SemaphoreType.DMA((2 * (cols // LANES),)),
             ],
             compiler_params=room,
             name="new_momentum_and_update",

time: 40.6 us -> 40.6 us (level)
  no operation moved by 1% of the time
where the time goes in v9:
time: 40.6 us; the launch traced here: 40.3 us
  blocking collectives  23.6 us (58%)
  starting transfers between devices  11.3 us (28%)
  Pallas kernels  4.6 us (11%)
  between operations  0.65 us (2%)
    all_to_all x1, blocking collectives, exchange(): return lax.all_to_all(x, axes, 0, 0, axis_index_groups=groups, tiled=True)  19.3 us
    all_to_all x1, starting transfers between devices, exchange(): return lax.all_to_all(x, axes, 0, 0, axis_index_groups=groups, tiled=True)  11.3 us
    all_gather x1, blocking collectives, per_device(): total = lax.all_gather(jnp.sum(got, axis=0), 'core', tiled=True)  2.45 us
    all_gather x1, blocking collectives, per_device(): coded = lax.all_gather(coded, 'core')  1.86 us
    pallas_call x1, Pallas kernels, per_device(): pl.pallas_call(first_kernel, in_specs=[pl.BlockSpec(memory_space=pltpu.HB...  1.68 us
    pallas_call x1, Pallas kernels, per_device(): pl.pallas_call(last_kernel, out_shape=(pltpu.HBM(momentum.shape, f32), pl...  1.44 us
    pallas_call x1, Pallas kernels, per_device(): pl.pallas_call(code_kernel, out_shape=vmem(((8, cols), f32), (momentum.sh...  1.3 us
  transfers between devices with their start and end apart: 1, of which 1 were waited for; matrix products, arithmetic and copies ran while one was open for 0% of the time, Pallas kernels for 3%

profile of v9, /device:TPU:1, one launch (start us, length us, event | category | flops | bytes accessed | tf_op | source)
XLA Modules:
  0.0 40.3 jit_solution(16585750474507403728)
XLA Ops:
  0.6 1.7 %squares.1 = (f32[16,2,128]{2,1,0:T(2,128)}, f32[1,2,128,640]{3,2,1,0:T(8,128)S(1)}, bf16[1,2,128,640]{3,2,1,0:T(8,128)(2,1)S(1)}, f32[64,128]{1,0:T(8,128)S(1)}...) custom-call(f32[1,2,128,640]{3,2,1,0:T(8,128)} %mom_hbm.1, bf16[1,2,128,640]{3,2,1,0:T(8,128)(2,1)} %grad_hbm.1, ...), custom_call_target="tpu_custom_call" | custom-call | tf_op jit(solution)/shard_map/squares/pallas_call | solution.py:185
  2.3 11.3 %all-to-all-start = ((f32[16,2,128]{2,1,0:T(2,128)}), f32[16,2,128]{2,1,0:T(2,128)S(1)}, u32[]{:S(2)}, u32[]{:S(2)}) async-start(f32[16,2,128]{2,1,0:T(2,128)} %get-tuple-element.20), calls=%async_computation | async-start | bytes 32768 | tf_op jit(solution)/shard_map/all_to_all | solution.py:166
  13.7 1.3 %transforms.1 = (f32[8,640]{1,0:T(8,128)S(1)}, f32[1,2,128,640]{3,2,1,0:T(8,128)S(1)}, f32[1,2,128,640]{3,2,1,0:T(8,128)S(1)}) custom-call(f32[1,2,128,640]{3,2,1,0:T(8,128)S(1)} %get-tuple-element.13.mom_ref, bf16[1,2,128,640]{3,2,1,0:T(8,128)(2,1)S(1)} %get-tuple-element.14.grad_ref, f32[64,128]{1,0:T(8,128)S(1)} %get-tuple-element.15.pick_ref, ...), custom_call_target="tpu_custom_call" | custom-call | flops 268435456 | bytes 4194304 | tf_op jit(solution)/shard_map/transforms/pallas_call | solution.py:201
  15.0 1.9 %all-gather = f32[16,640]{1,0:T(8,128)S(1)} all-gather(f32[8,640]{1,0:T(8,128)S(1)} %get-tuple-element.21), channel_id=2, replica_groups=mesh['z'=8,'yh'=4,'core'=2,'yl'=2,'x'=4] {'core'}, dimensions={0}, use_global_device_ids=true | all-gather | bytes 61440 | tf_op jit(solution)/shard_map/all_gather | solution.py:209
  16.8 0.1 all-to-all-done.refs_0_
  16.9 0.2 spectra.1
  17.1 19.3 %all_to_all.10 = f32[32,2,640]{2,1,0:T(2,128)S(1)} all-to-all(f32[32,2,640]{2,1,0:T(2,128)S(1)} %get-tuple-element.23), channel_id=1, replica_groups={{416,432,384,400,480,496,448,464,32,48,0,16,96,112,64,80,160,176,128,14..., dimensions={0} | all-to-all | bytes 327680 | tf_op jit(solution)/shard_map/all_to_all | solution.py:166
  36.4 0.1 reduce_sum.9
  36.4 2.4 %all-gather.1 = f32[2,2,640]{2,1,0:T(2,128)S(1)} all-gather(f32[1,2,640]{2,1,0:T(2,128)S(1)} %bitcast.4), channel_id=1, replica_groups=mesh['z'=8,'yh'=4,'core'=2,'yl'=2,'x'=4] {'core'}, dimensions={0}, use_global_device_ids=true | all-gather | bytes 15360 | tf_op jit(solution)/shard_map/all_gather | solution.py:218
  38.9 1.4 %new_momentum_and_update.1 = (f32[1,2,128,640]{3,2,1,0:T(8,128)}, bf16[2,128,640]{2,1,0:T(8,128)(2,1)}) custom-call(f32[1,2,128,640]{3,2,1,0:T(8,128)S(1)} %get-tuple-element.18.rest_mom_ref, f32[1,2,128,640]{3,2,1,0:T(8,128)S(1)} %get-tuple-element.19.rest_grad_ref, f32[8,128]{1,0:T(8,128)S(1)} %get-tuple-element.22.clip_ref, ...), custom_call_target="tpu_custom_call" | custom-call | tf_op jit(solution)/shard_map/new_momentum_and_update/pallas_call | solution.py:219
  (1 shorter events, 0.0 us)
Async XLA Ops:
  2.3 14.6 %all-to-all-start = ((f32[16,2,128]{2,1,0:T(2,128)}), f32[16,2,128]{2,1,0:T(2,128)S(1)}, u32[]{:S(2)}, u32[]{:S(2)}) async-start(f32[16,2,128]{2,1,0:T(2,128)} %get-tuple-element.20), calls=%async_computation | async-start | bytes 32768 | tf_op jit(solution)/shard_map/all_to_all | solution.py:166
